TPU v7x, 256 devices: a whole 4x4x8 slice. The times are simulated.
256 devices in a mesh: section: 8 (over y, core), seq: 32 (over x, z).
Axes of the slice: x: 4, y: 4, z: 8, core: 2. Of those that a mesh axis runs over, the one named last changes fastest.
Arguments:
- queries: bfloat16 [8, 4096, 2048], P('section', 'seq'), may hold values from -4 to 4
- memory_keys: bfloat16 [8, 4096, 2048], P('section', 'seq'), may hold values from -2.5 to 2.5
- memory_values: bfloat16 [8, 4096, 2048], P('section', 'seq'), may hold values from -4 to 4
- upstream: bfloat16 [8, 4096, 2048], P('section', 'seq'), may hold values from -4 to 4
- inner_rate: float32 [8, 32], P('section'), may hold values from 0.02 to 0.2
- checkpoints: float32 [8, 32, 32, 4096], P('section', 'seq'), may hold values from -0.75 to 0.75
Outputs:
- grad_queries: bfloat16 [8, 4096, 2048], P('section', 'seq')
- grad_keys: bfloat16 [8, 4096, 2048], P('section', 'seq')
- grad_values: bfloat16 [8, 4096, 2048], P('section', 'seq')
- adjoint_start: float32 [8, 32, 32, 4096], P('section', 'seq')
All inputs are finite; a program needn't handle non-finite values.
Results may differ from a plain program's by a relative error of at most 0.001.
Values may be sent and summed in bfloat16 or wider, within the bound.
No kernel may reach another device: no remote copies, remote signals or barrier semaphores. Data moves between devices by JAX's collectives and lax.ppermute only.
A program may use at most 128 MiB of HBM per device.

v0:
```python
from functools import partial

import jax
import jax.numpy as jnp
from jax import lax
from jax.sharding import PartitionSpec as P

MB = 64


inner_product = partial(jnp.einsum, precision=lax.Precision.HIGHEST)


def passed_along(block, axis, distance):
    devices = range(lax.axis_size(axis))
    route = [((i - distance) % len(devices), i) for i in devices]
    return lax.ppermute(block, axis, route)


def shifted(value, axis, steps):
    count = lax.axis_size(axis)
    initial, last = (max(0, -steps), min(count, count - steps))
    return lax.ppermute(value, axis, [(source, source + steps) for source in range(initial, last)])


def lower_mask(length):
    row_index = lax.broadcasted_iota(jnp.int32, (length, length), 0)
    col_index = lax.broadcasted_iota(jnp.int32, (length, length), 1)
    return (row_index >= col_index).astype(jnp.float32)


def per_device(queries, memory_keys, memory_values, upstream, inner_rate, checkpoints):
    head_count = inner_rate.shape[1]
    feature_count = queries.shape[2]
    head_size = feature_count // head_count
    tokens = queries.shape[1]
    block_count = tokens // MB

    def to_blocks(array):
        shaped = array[0].astype(jnp.float32).reshape(block_count, MB, head_count, head_size)
        return jnp.transpose(shaped, (0, 2, 1, 3))

    def from_blocks(array):
        return (
            jnp.transpose(array, (0, 2, 1, 3))
            .reshape(1, tokens, feature_count)
            .astype(jnp.bfloat16)
        )

    update_rate = (inner_rate[0] / MB)[:, None, None]
    masked_scores = lower_mask(MB)
    initial = checkpoints[0, 0].reshape(head_count, head_size, head_size)
    key_blocks = to_blocks(memory_keys)
    value_blocks = to_blocks(memory_values)

    def forward(weight_stack, operands):
        current_key, current_value = operands
        error_rows = inner_product("ick,iku->icu", current_key, weight_stack) - current_value
        updated_weight = weight_stack - update_rate * inner_product(
            "fwl,fwn->fln", current_key, error_rows
        )
        return (updated_weight, (weight_stack, error_rows))

    weight_trail, error_trail = lax.scan(forward, initial, (key_blocks, value_blocks))[1]
    cotangent = passed_along(upstream, "section", -1)
    query_blocks = to_blocks(queries)
    grad_blocks = to_blocks(cotangent)
    identity_map = jnp.broadcast_to(
        jnp.eye(head_size, dtype=jnp.float32), (head_count, head_size, head_size)
    )
    empty = jnp.zeros((head_count, head_size, head_size), jnp.float32)

    def compose(stacked, operands):
        current_query, current_key, current_gradient = operands
        attention_scores = inner_product("sxi,sbi->sxb", current_query, current_key) * masked_scores
        carried = inner_product("hmn,hme->hne", attention_scores, current_gradient)
        source_weight = inner_product(
            "fwl,fwn->fln", current_query, current_gradient
        ) - update_rate * inner_product("wik,wiy->wky", current_key, carried)
        projected = inner_product("hnd,hde->hne", current_key, stacked)
        stacked = stacked - update_rate * inner_product("wik,wiy->wky", current_key, projected)
        stacked = stacked + jnp.concatenate([empty, source_weight], axis=2)
        return (stacked, (carried, source_weight))

    stacked, (carried_trail, source_trail) = lax.scan(
        compose,
        jnp.concatenate([identity_map, empty], axis=2),
        (query_blocks, key_blocks, grad_blocks),
        reverse=True,
    )
    linear = stacked[:, :, :head_size]
    offset = stacked[:, :, head_size:]
    shard_count = lax.axis_size("seq")

    def advance(position, adjoint_end):
        shard_begin = inner_product("hde,hef->hdf", linear, adjoint_end) + offset
        return shifted(shard_begin, "seq", -1)

    adjoint_end = lax.fori_loop(0, shard_count - 1, advance, empty)

    def backward(adjoint_carry, operands):
        (
            current_query,
            current_key,
            current_gradient,
            current_weight,
            error_now,
            carried,
            source_weight,
        ) = operands
        projected = inner_product("hnd,hde->hne", current_key, adjoint_carry)
        error_gradient = -update_rate * (carried + projected)
        score_gradient = (
            -update_rate
            * inner_product("hme,hne->hmn", current_gradient, error_now)
            * masked_scores
        )
        query_gradient = inner_product(
            "nyv,nxv->nyx", current_gradient, current_weight
        ) + inner_product("clo,coq->clq", score_gradient, current_key)
        grad_key = (
            inner_product("hne,hde->hnd", error_gradient, current_weight)
            - update_rate * inner_product("hne,hde->hnd", error_now, adjoint_carry)
            + inner_product("fbw,fbe->fwe", score_gradient, current_query)
        )
        previous_weight = (
            adjoint_carry
            + source_weight
            - update_rate * inner_product("wik,wiy->wky", current_key, projected)
        )
        return (previous_weight, (query_gradient, grad_key, -error_gradient))

    shard_start, (query_grads, key_grads, value_grads) = lax.scan(
        backward,
        adjoint_end,
        (
            query_blocks,
            key_blocks,
            grad_blocks,
            weight_trail,
            error_trail,
            carried_trail,
            source_trail,
        ),
        reverse=True,
    )
    adjoint_start = shard_start.reshape(1, 1, head_count, head_size * head_size)
    return (
        from_blocks(query_grads),
        from_blocks(key_grads),
        from_blocks(value_grads),
        adjoint_start,
    )


def solution(mesh):
    return jax.shard_map(
        per_device,
        mesh=mesh,
        in_specs=(
            P("section", "seq", None),
            P("section", "seq", None),
            P("section", "seq", None),
            P("section", "seq", None),
            P("section", None),
            P("section", "seq", None, None),
        ),
        out_specs=(
            P("section", "seq", None),
            P("section", "seq", None),
            P("section", "seq", None),
            P("section", "seq", None, None),
        ),
        check_vma=False,
    )
```

profile of v0, /device:TPU:22, one launch (start us, length us, event | category | flops | bytes accessed | tf_op | source)
XLA Modules:
  0.0 1025.3 jit_solution(10809559419235036649)
XLA Ops:
  42.3 41.1 %while.66 = (s32[]{:T(128)}, f32[32,64,128]{2,1,0:T(8,128)}, f32[2,32,64,64]{3,2,1,0:T(8,128)}, f32[2,32,64,64]{3,2,1,0:T(8,128)}, f32[32,1,1]{0,2,1:T(1,128)S(1...) while((s32[]{:T(128)}, f32[32,64,128]{2,1,0:T(8,128)}, ...), condition=%wide.region_1.2_spmd.clone, body=%wide.region_0.1_spmd.clone.sunk | while | flops 806494208 | bytes 47220636 | solution.py:85
  86.7 891.8 %while.64 = (s32[]{:T(128)}, f32[32,64,64]{2,1,0:T(8,128)S(1)}, f32[32,64,64]{2,1,0:T(8,128)}, f32[32,64,64]{2,1,0:T(8,128)}, s32[]{:T(128)}) while((s32[]{:T(128)}, f32[32,64,64]{2,1,0:T(8,128)S(1)}, f32[32,64,64]{2,1,0:T(8,128)}, f32[32,64,64]{2,1,0:T(8,128)}, s32[]{:T(128)}) %tuple.124), condition=%wide.region_3.4_spmd, body=%wide.region_2.3_spmd.sunk | while | flops 100794368 | bytes 4194405 | solution.py:99
  98.4 23.4 %collective-permute-done = f32[32,64,64]{2,1,0:T(8,128)S(1)} collective-permute-done((f32[32,64,64]{2,1,0:T(8,128)}, f32[32,64,64]{2,1,0:T(8,128)S(1)}, u32[]{:S(2)}, u32[]{:S(2)}) %collective-permute-start) | collective-permute-done | bytes 524320 | tf_op jit(solution)/shard_map/while/body/eval_jaxpr/ppermute | solution.py:23
  131.9 22.6 %collective-permute-done = f32[32,64,64]{2,1,0:T(8,128)S(1)} collective-permute-done((f32[32,64,64]{2,1,0:T(8,128)}, f32[32,64,64]{2,1,0:T(8,128)S(1)}, u32[]{:S(2)}, u32[]{:S(2)}) %collective-permute-start) | collective-permute-done | bytes 524320 | tf_op jit(solution)/shard_map/while/body/eval_jaxpr/ppermute | solution.py:23
  164.5 21.7 %collective-permute-done = f32[32,64,64]{2,1,0:T(8,128)S(1)} collective-permute-done((f32[32,64,64]{2,1,0:T(8,128)}, f32[32,64,64]{2,1,0:T(8,128)S(1)}, u32[]{:S(2)}, u32[]{:S(2)}) %collective-permute-start) | collective-permute-done | bytes 524320 | tf_op jit(solution)/shard_map/while/body/eval_jaxpr/ppermute | solution.py:23
  196.3 20.8 %collective-permute-done = f32[32,64,64]{2,1,0:T(8,128)S(1)} collective-permute-done((f32[32,64,64]{2,1,0:T(8,128)}, f32[32,64,64]{2,1,0:T(8,128)S(1)}, u32[]{:S(2)}, u32[]{:S(2)}) %collective-permute-start) | collective-permute-done | bytes 524320 | tf_op jit(solution)/shard_map/while/body/eval_jaxpr/ppermute | solution.py:23
  227.1 19.9 %collective-permute-done = f32[32,64,64]{2,1,0:T(8,128)S(1)} collective-permute-done((f32[32,64,64]{2,1,0:T(8,128)}, f32[32,64,64]{2,1,0:T(8,128)S(1)}, u32[]{:S(2)}, u32[]{:S(2)}) %collective-permute-start) | collective-permute-done | bytes 524320 | tf_op jit(solution)/shard_map/while/body/eval_jaxpr/ppermute | solution.py:23
  257.0 18.9 %collective-permute-done = f32[32,64,64]{2,1,0:T(8,128)S(1)} collective-permute-done((f32[32,64,64]{2,1,0:T(8,128)}, f32[32,64,64]{2,1,0:T(8,128)S(1)}, u32[]{:S(2)}, u32[]{:S(2)}) %collective-permute-start) | collective-permute-done | bytes 524320 | tf_op jit(solution)/shard_map/while/body/eval_jaxpr/ppermute | solution.py:23
  286.0 18.0 %collective-permute-done = f32[32,64,64]{2,1,0:T(8,128)S(1)} collective-permute-done((f32[32,64,64]{2,1,0:T(8,128)}, f32[32,64,64]{2,1,0:T(8,128)S(1)}, u32[]{:S(2)}, u32[]{:S(2)}) %collective-permute-start) | collective-permute-done | bytes 524320 | tf_op jit(solution)/shard_map/while/body/eval_jaxpr/ppermute | solution.py:23
  314.1 17.1 %collective-permute-done = f32[32,64,64]{2,1,0:T(8,128)S(1)} collective-permute-done((f32[32,64,64]{2,1,0:T(8,128)}, f32[32,64,64]{2,1,0:T(8,128)S(1)}, u32[]{:S(2)}, u32[]{:S(2)}) %collective-permute-start) | collective-permute-done | bytes 524320 | tf_op jit(solution)/shard_map/while/body/eval_jaxpr/ppermute | solution.py:23
  341.3 16.2 %collective-permute-done = f32[32,64,64]{2,1,0:T(8,128)S(1)} collective-permute-done((f32[32,64,64]{2,1,0:T(8,128)}, f32[32,64,64]{2,1,0:T(8,128)S(1)}, u32[]{:S(2)}, u32[]{:S(2)}) %collective-permute-start) | collective-permute-done | bytes 524320 | tf_op jit(solution)/shard_map/while/body/eval_jaxpr/ppermute | solution.py:23
  367.5 15.2 %collective-permute-done = f32[32,64,64]{2,1,0:T(8,128)S(1)} collective-permute-done((f32[32,64,64]{2,1,0:T(8,128)}, f32[32,64,64]{2,1,0:T(8,128)S(1)}, u32[]{:S(2)}, u32[]{:S(2)}) %collective-permute-start) | collective-permute-done | bytes 524320 | tf_op jit(solution)/shard_map/while/body/eval_jaxpr/ppermute | solution.py:23
  392.8 14.3 %collective-permute-done = f32[32,64,64]{2,1,0:T(8,128)S(1)} collective-permute-done((f32[32,64,64]{2,1,0:T(8,128)}, f32[32,64,64]{2,1,0:T(8,128)S(1)}, u32[]{:S(2)}, u32[]{:S(2)}) %collective-permute-start) | collective-permute-done | bytes 524320 | tf_op jit(solution)/shard_map/while/body/eval_jaxpr/ppermute | solution.py:23
  440.6 13.6 %collective-permute-done = f32[32,64,64]{2,1,0:T(8,128)S(1)} collective-permute-done((f32[32,64,64]{2,1,0:T(8,128)}, f32[32,64,64]{2,1,0:T(8,128)S(1)}, u32[]{:S(2)}, u32[]{:S(2)}) %collective-permute-start) | collective-permute-done | bytes 524320 | tf_op jit(solution)/shard_map/while/body/eval_jaxpr/ppermute | solution.py:23
  464.3 14.7 %collective-permute-done = f32[32,64,64]{2,1,0:T(8,128)S(1)} collective-permute-done((f32[32,64,64]{2,1,0:T(8,128)}, f32[32,64,64]{2,1,0:T(8,128)S(1)}, u32[]{:S(2)}, u32[]{:S(2)}) %collective-permute-start) | collective-permute-done | bytes 524320 | tf_op jit(solution)/shard_map/while/body/eval_jaxpr/ppermute | solution.py:23
  489.1 15.8 %collective-permute-done = f32[32,64,64]{2,1,0:T(8,128)S(1)} collective-permute-done((f32[32,64,64]{2,1,0:T(8,128)}, f32[32,64,64]{2,1,0:T(8,128)S(1)}, u32[]{:S(2)}, u32[]{:S(2)}) %collective-permute-start) | collective-permute-done | bytes 524320 | tf_op jit(solution)/shard_map/while/body/eval_jaxpr/ppermute | solution.py:23
  514.9 16.9 %collective-permute-done = f32[32,64,64]{2,1,0:T(8,128)S(1)} collective-permute-done((f32[32,64,64]{2,1,0:T(8,128)}, f32[32,64,64]{2,1,0:T(8,128)S(1)}, u32[]{:S(2)}, u32[]{:S(2)}) %collective-permute-start) | collective-permute-done | bytes 524320 | tf_op jit(solution)/shard_map/while/body/eval_jaxpr/ppermute | solution.py:23
  541.8 17.9 %collective-permute-done = f32[32,64,64]{2,1,0:T(8,128)S(1)} collective-permute-done((f32[32,64,64]{2,1,0:T(8,128)}, f32[32,64,64]{2,1,0:T(8,128)S(1)}, u32[]{:S(2)}, u32[]{:S(2)}) %collective-permute-start) | collective-permute-done | bytes 524320 | tf_op jit(solution)/shard_map/while/body/eval_jaxpr/ppermute | solution.py:23
  569.8 19.0 %collective-permute-done = f32[32,64,64]{2,1,0:T(8,128)S(1)} collective-permute-done((f32[32,64,64]{2,1,0:T(8,128)}, f32[32,64,64]{2,1,0:T(8,128)S(1)}, u32[]{:S(2)}, u32[]{:S(2)}) %collective-permute-start) | collective-permute-done | bytes 524320 | tf_op jit(solution)/shard_map/while/body/eval_jaxpr/ppermute | solution.py:23
  598.9 20.1 %collective-permute-done = f32[32,64,64]{2,1,0:T(8,128)S(1)} collective-permute-done((f32[32,64,64]{2,1,0:T(8,128)}, f32[32,64,64]{2,1,0:T(8,128)S(1)}, u32[]{:S(2)}, u32[]{:S(2)}) %collective-permute-start) | collective-permute-done | bytes 524320 | tf_op jit(solution)/shard_map/while/body/eval_jaxpr/ppermute | solution.py:23
  629.1 21.2 %collective-permute-done = f32[32,64,64]{2,1,0:T(8,128)S(1)} collective-permute-done((f32[32,64,64]{2,1,0:T(8,128)}, f32[32,64,64]{2,1,0:T(8,128)S(1)}, u32[]{:S(2)}, u32[]{:S(2)}) %collective-permute-start) | collective-permute-done | bytes 524320 | tf_op jit(solution)/shard_map/while/body/eval_jaxpr/ppermute | solution.py:23
  660.3 22.3 %collective-permute-done = f32[32,64,64]{2,1,0:T(8,128)S(1)} collective-permute-done((f32[32,64,64]{2,1,0:T(8,128)}, f32[32,64,64]{2,1,0:T(8,128)S(1)}, u32[]{:S(2)}, u32[]{:S(2)}) %collective-permute-start) | collective-permute-done | bytes 524320 | tf_op jit(solution)/shard_map/while/body/eval_jaxpr/ppermute | solution.py:23
  692.7 23.5 %collective-permute-done = f32[32,64,64]{2,1,0:T(8,128)S(1)} collective-permute-done((f32[32,64,64]{2,1,0:T(8,128)}, f32[32,64,64]{2,1,0:T(8,128)S(1)}, u32[]{:S(2)}, u32[]{:S(2)}) %collective-permute-start) | collective-permute-done | bytes 524320 | tf_op jit(solution)/shard_map/while/body/eval_jaxpr/ppermute | solution.py:23
  726.2 23.0 %collective-permute-done = f32[32,64,64]{2,1,0:T(8,128)S(1)} collective-permute-done((f32[32,64,64]{2,1,0:T(8,128)}, f32[32,64,64]{2,1,0:T(8,128)S(1)}, u32[]{:S(2)}, u32[]{:S(2)}) %collective-permute-start) | collective-permute-done | bytes 524320 | tf_op jit(solution)/shard_map/while/body/eval_jaxpr/ppermute | solution.py:23
  759.3 22.2 %collective-permute-done = f32[32,64,64]{2,1,0:T(8,128)S(1)} collective-permute-done((f32[32,64,64]{2,1,0:T(8,128)}, f32[32,64,64]{2,1,0:T(8,128)S(1)}, u32[]{:S(2)}, u32[]{:S(2)}) %collective-permute-start) | collective-permute-done | bytes 524320 | tf_op jit(solution)/shard_map/while/body/eval_jaxpr/ppermute | solution.py:23
  791.6 21.3 %collective-permute-done = f32[32,64,64]{2,1,0:T(8,128)S(1)} collective-permute-done((f32[32,64,64]{2,1,0:T(8,128)}, f32[32,64,64]{2,1,0:T(8,128)S(1)}, u32[]{:S(2)}, u32[]{:S(2)}) %collective-permute-start) | collective-permute-done | bytes 524320 | tf_op jit(solution)/shard_map/while/body/eval_jaxpr/ppermute | solution.py:23
  823.0 20.4 %collective-permute-done = f32[32,64,64]{2,1,0:T(8,128)S(1)} collective-permute-done((f32[32,64,64]{2,1,0:T(8,128)}, f32[32,64,64]{2,1,0:T(8,128)S(1)}, u32[]{:S(2)}, u32[]{:S(2)}) %collective-permute-start) | collective-permute-done | bytes 524320 | tf_op jit(solution)/shard_map/while/body/eval_jaxpr/ppermute | solution.py:23
  853.4 19.5 %collective-permute-done = f32[32,64,64]{2,1,0:T(8,128)S(1)} collective-permute-done((f32[32,64,64]{2,1,0:T(8,128)}, f32[32,64,64]{2,1,0:T(8,128)S(1)}, u32[]{:S(2)}, u32[]{:S(2)}) %collective-permute-start) | collective-permute-done | bytes 524320 | tf_op jit(solution)/shard_map/while/body/eval_jaxpr/ppermute | solution.py:23
  882.9 18.5 %collective-permute-done = f32[32,64,64]{2,1,0:T(8,128)S(1)} collective-permute-done((f32[32,64,64]{2,1,0:T(8,128)}, f32[32,64,64]{2,1,0:T(8,128)S(1)}, u32[]{:S(2)}, u32[]{:S(2)}) %collective-permute-start) | collective-permute-done | bytes 524320 | tf_op jit(solution)/shard_map/while/body/eval_jaxpr/ppermute | solution.py:23
  911.5 17.6 %collective-permute-done = f32[32,64,64]{2,1,0:T(8,128)S(1)} collective-permute-done((f32[32,64,64]{2,1,0:T(8,128)}, f32[32,64,64]{2,1,0:T(8,128)S(1)}, u32[]{:S(2)}, u32[]{:S(2)}) %collective-permute-start) | collective-permute-done | bytes 524320 | tf_op jit(solution)/shard_map/while/body/eval_jaxpr/ppermute | solution.py:23
  939.2 16.7 %collective-permute-done = f32[32,64,64]{2,1,0:T(8,128)S(1)} collective-permute-done((f32[32,64,64]{2,1,0:T(8,128)}, f32[32,64,64]{2,1,0:T(8,128)S(1)}, u32[]{:S(2)}, u32[]{:S(2)}) %collective-permute-start) | collective-permute-done | bytes 524320 | tf_op jit(solution)/shard_map/while/body/eval_jaxpr/ppermute | solution.py:23
  978.5 34.9 %while.67 = (s32[]{:T(128)}, f32[32,64,64]{2,1,0:T(8,128)S(1)}, bf16[2,32,64,64]{3,2,1,0:T(8,128)(2,1)}, bf16[2,32,64,64]{3,2,1,0:T(8,128)(2,1)}, bf16[2,32,64,6...) while((s32[]{:T(128)}, f32[32,64,64]{2,1,0:T(8,128)S(1)}, ...), condition=%wide.region_7.8_spmd.clone, body=%wide.region_6.7_spmd.clone.sunk | while | flops 807149568 | bytes 63497148 | solution.py:133
  (235 shorter events, 481.8 us)
Async XLA Ops:
  0.6 31.2 %collective-permute-start.1 = (bf16[1,128,2048]{2,1,0:T(8,128)(2,1)}, bf16[1,128,2048]{2,1,0:T(8,128)(2,1)}, u32[]{:S(2)}, u32[]{:S(2)}) collective-permute-start(bf16[1,128,2048]{2,1,0:T(8,128)(2,1)} %param.17), channel_id=1, source_target_pairs={{32,0},{64,32},{96,64},{128,96},{160,128},{192,160},{224,192},{0,2... | collective-permute-start | bytes 1572872 | tf_op jit(solution)/shard_map/ppermute | solution.py:17
  90.4 31.4 %collective-permute-start = (f32[32,64,64]{2,1,0:T(8,128)}, f32[32,64,64]{2,1,0:T(8,128)S(1)}, u32[]{:S(2)}, u32[]{:S(2)}) collective-permute-start(f32[32,64,64]{2,1,0:T(8,128)} %convolution_add_fusion.4), channel_id=1, source_target_pairs={{1,0},{2,1},{3,2},{4,3},{5,4},{6,5},{7,6},{8,7},{9,8},{10,9},{11,1... | collective-permute-start | bytes 1572872 | tf_op jit(solution)/shard_map/while/body/eval_jaxpr/ppermute | solution.py:23
  125.5 29.0 %collective-permute-start = (f32[32,64,64]{2,1,0:T(8,128)}, f32[32,64,64]{2,1,0:T(8,128)S(1)}, u32[]{:S(2)}, u32[]{:S(2)}) collective-permute-start(f32[32,64,64]{2,1,0:T(8,128)} %convolution_add_fusion.4), channel_id=1, source_target_pairs={{1,0},{2,1},{3,2},{4,3},{5,4},{6,5},{7,6},{8,7},{9,8},{10,9},{11,1... | collective-permute-start | bytes 1572872 | tf_op jit(solution)/shard_map/while/body/eval_jaxpr/ppermute | solution.py:23
  158.1 28.1 %collective-permute-start = (f32[32,64,64]{2,1,0:T(8,128)}, f32[32,64,64]{2,1,0:T(8,128)S(1)}, u32[]{:S(2)}, u32[]{:S(2)}) collective-permute-start(f32[32,64,64]{2,1,0:T(8,128)} %convolution_add_fusion.4), channel_id=1, source_target_pairs={{1,0},{2,1},{3,2},{4,3},{5,4},{6,5},{7,6},{8,7},{9,8},{10,9},{11,1... | collective-permute-start | bytes 1572872 | tf_op jit(solution)/shard_map/while/body/eval_jaxpr/ppermute | solution.py:23
  189.9 27.2 %collective-permute-start = (f32[32,64,64]{2,1,0:T(8,128)}, f32[32,64,64]{2,1,0:T(8,128)S(1)}, u32[]{:S(2)}, u32[]{:S(2)}) collective-permute-start(f32[32,64,64]{2,1,0:T(8,128)} %convolution_add_fusion.4), channel_id=1, source_target_pairs={{1,0},{2,1},{3,2},{4,3},{5,4},{6,5},{7,6},{8,7},{9,8},{10,9},{11,1... | collective-permute-start | bytes 1572872 | tf_op jit(solution)/shard_map/while/body/eval_jaxpr/ppermute | solution.py:23
  220.7 26.2 %collective-permute-start = (f32[32,64,64]{2,1,0:T(8,128)}, f32[32,64,64]{2,1,0:T(8,128)S(1)}, u32[]{:S(2)}, u32[]{:S(2)}) collective-permute-start(f32[32,64,64]{2,1,0:T(8,128)} %convolution_add_fusion.4), channel_id=1, source_target_pairs={{1,0},{2,1},{3,2},{4,3},{5,4},{6,5},{7,6},{8,7},{9,8},{10,9},{11,1... | collective-permute-start | bytes 1572872 | tf_op jit(solution)/shard_map/while/body/eval_jaxpr/ppermute | solution.py:23
  250.6 25.3 %collective-permute-start = (f32[32,64,64]{2,1,0:T(8,128)}, f32[32,64,64]{2,1,0:T(8,128)S(1)}, u32[]{:S(2)}, u32[]{:S(2)}) collective-permute-start(f32[32,64,64]{2,1,0:T(8,128)} %convolution_add_fusion.4), channel_id=1, source_target_pairs={{1,0},{2,1},{3,2},{4,3},{5,4},{6,5},{7,6},{8,7},{9,8},{10,9},{11,1... | collective-permute-start | bytes 1572872 | tf_op jit(solution)/shard_map/while/body/eval_jaxpr/ppermute | solution.py:23
  279.6 24.4 %collective-permute-start = (f32[32,64,64]{2,1,0:T(8,128)}, f32[32,64,64]{2,1,0:T(8,128)S(1)}, u32[]{:S(2)}, u32[]{:S(2)}) collective-permute-start(f32[32,64,64]{2,1,0:T(8,128)} %convolution_add_fusion.4), channel_id=1, source_target_pairs={{1,0},{2,1},{3,2},{4,3},{5,4},{6,5},{7,6},{8,7},{9,8},{10,9},{11,1... | collective-permute-start | bytes 1572872 | tf_op jit(solution)/shard_map/while/body/eval_jaxpr/ppermute | solution.py:23
  307.7 23.5 %collective-permute-start = (f32[32,64,64]{2,1,0:T(8,128)}, f32[32,64,64]{2,1,0:T(8,128)S(1)}, u32[]{:S(2)}, u32[]{:S(2)}) collective-permute-start(f32[32,64,64]{2,1,0:T(8,128)} %convolution_add_fusion.4), channel_id=1, source_target_pairs={{1,0},{2,1},{3,2},{4,3},{5,4},{6,5},{7,6},{8,7},{9,8},{10,9},{11,1... | collective-permute-start | bytes 1572872 | tf_op jit(solution)/shard_map/while/body/eval_jaxpr/ppermute | solution.py:23
  334.9 22.6 %collective-permute-start = (f32[32,64,64]{2,1,0:T(8,128)}, f32[32,64,64]{2,1,0:T(8,128)S(1)}, u32[]{:S(2)}, u32[]{:S(2)}) collective-permute-start(f32[32,64,64]{2,1,0:T(8,128)} %convolution_add_fusion.4), channel_id=1, source_target_pairs={{1,0},{2,1},{3,2},{4,3},{5,4},{6,5},{7,6},{8,7},{9,8},{10,9},{11,1... | collective-permute-start | bytes 1572872 | tf_op jit(solution)/shard_map/while/body/eval_jaxpr/ppermute | solution.py:23
  361.1 21.6 %collective-permute-start = (f32[32,64,64]{2,1,0:T(8,128)}, f32[32,64,64]{2,1,0:T(8,128)S(1)}, u32[]{:S(2)}, u32[]{:S(2)}) collective-permute-start(f32[32,64,64]{2,1,0:T(8,128)} %convolution_add_fusion.4), channel_id=1, source_target_pairs={{1,0},{2,1},{3,2},{4,3},{5,4},{6,5},{7,6},{8,7},{9,8},{10,9},{11,1... | collective-permute-start | bytes 1572872 | tf_op jit(solution)/shard_map/while/body/eval_jaxpr/ppermute | solution.py:23
  386.4 20.7 %collective-permute-start = (f32[32,64,64]{2,1,0:T(8,128)}, f32[32,64,64]{2,1,0:T(8,128)S(1)}, u32[]{:S(2)}, u32[]{:S(2)}) collective-permute-start(f32[32,64,64]{2,1,0:T(8,128)} %convolution_add_fusion.4), channel_id=1, source_target_pairs={{1,0},{2,1},{3,2},{4,3},{5,4},{6,5},{7,6},{8,7},{9,8},{10,9},{11,1... | collective-permute-start | bytes 1572872 | tf_op jit(solution)/shard_map/while/body/eval_jaxpr/ppermute | solution.py:23
  410.8 19.8 %collective-permute-start = (f32[32,64,64]{2,1,0:T(8,128)}, f32[32,64,64]{2,1,0:T(8,128)S(1)}, u32[]{:S(2)}, u32[]{:S(2)}) collective-permute-start(f32[32,64,64]{2,1,0:T(8,128)} %convolution_add_fusion.4), channel_id=1, source_target_pairs={{1,0},{2,1},{3,2},{4,3},{5,4},{6,5},{7,6},{8,7},{9,8},{10,9},{11,1... | collective-permute-start | bytes 1572872 | tf_op jit(solution)/shard_map/while/body/eval_jaxpr/ppermute | solution.py:23
  434.3 20.0 %collective-permute-start = (f32[32,64,64]{2,1,0:T(8,128)}, f32[32,64,64]{2,1,0:T(8,128)S(1)}, u32[]{:S(2)}, u32[]{:S(2)}) collective-permute-start(f32[32,64,64]{2,1,0:T(8,128)} %convolution_add_fusion.4), channel_id=1, source_target_pairs={{1,0},{2,1},{3,2},{4,3},{5,4},{6,5},{7,6},{8,7},{9,8},{10,9},{11,1... | collective-permute-start | bytes 1572872 | tf_op jit(solution)/shard_map/while/body/eval_jaxpr/ppermute | solution.py:23
  457.9 21.1 %collective-permute-start = (f32[32,64,64]{2,1,0:T(8,128)}, f32[32,64,64]{2,1,0:T(8,128)S(1)}, u32[]{:S(2)}, u32[]{:S(2)}) collective-permute-start(f32[32,64,64]{2,1,0:T(8,128)} %convolution_add_fusion.4), channel_id=1, source_target_pairs={{1,0},{2,1},{3,2},{4,3},{5,4},{6,5},{7,6},{8,7},{9,8},{10,9},{11,1... | collective-permute-start | bytes 1572872 | tf_op jit(solution)/shard_map/while/body/eval_jaxpr/ppermute | solution.py:23
  482.7 22.2 %collective-permute-start = (f32[32,64,64]{2,1,0:T(8,128)}, f32[32,64,64]{2,1,0:T(8,128)S(1)}, u32[]{:S(2)}, u32[]{:S(2)}) collective-permute-start(f32[32,64,64]{2,1,0:T(8,128)} %convolution_add_fusion.4), channel_id=1, source_target_pairs={{1,0},{2,1},{3,2},{4,3},{5,4},{6,5},{7,6},{8,7},{9,8},{10,9},{11,1... | collective-permute-start | bytes 1572872 | tf_op jit(solution)/shard_map/while/body/eval_jaxpr/ppermute | solution.py:23
  508.5 23.3 %collective-permute-start = (f32[32,64,64]{2,1,0:T(8,128)}, f32[32,64,64]{2,1,0:T(8,128)S(1)}, u32[]{:S(2)}, u32[]{:S(2)}) collective-permute-start(f32[32,64,64]{2,1,0:T(8,128)} %convolution_add_fusion.4), channel_id=1, source_target_pairs={{1,0},{2,1},{3,2},{4,3},{5,4},{6,5},{7,6},{8,7},{9,8},{10,9},{11,1... | collective-permute-start | bytes 1572872 | tf_op jit(solution)/shard_map/while/body/eval_jaxpr/ppermute | solution.py:23
  535.5 24.3 %collective-permute-start = (f32[32,64,64]{2,1,0:T(8,128)}, f32[32,64,64]{2,1,0:T(8,128)S(1)}, u32[]{:S(2)}, u32[]{:S(2)}) collective-permute-start(f32[32,64,64]{2,1,0:T(8,128)} %convolution_add_fusion.4), channel_id=1, source_target_pairs={{1,0},{2,1},{3,2},{4,3},{5,4},{6,5},{7,6},{8,7},{9,8},{10,9},{11,1... | collective-permute-start | bytes 1572872 | tf_op jit(solution)/shard_map/while/body/eval_jaxpr/ppermute | solution.py:23
  563.5 25.4 %collective-permute-start = (f32[32,64,64]{2,1,0:T(8,128)}, f32[32,64,64]{2,1,0:T(8,128)S(1)}, u32[]{:S(2)}, u32[]{:S(2)}) collective-permute-start(f32[32,64,64]{2,1,0:T(8,128)} %convolution_add_fusion.4), channel_id=1, source_target_pairs={{1,0},{2,1},{3,2},{4,3},{5,4},{6,5},{7,6},{8,7},{9,8},{10,9},{11,1... | collective-permute-start | bytes 1572872 | tf_op jit(solution)/shard_map/while/body/eval_jaxpr/ppermute | solution.py:23
  592.5 26.5 %collective-permute-start = (f32[32,64,64]{2,1,0:T(8,128)}, f32[32,64,64]{2,1,0:T(8,128)S(1)}, u32[]{:S(2)}, u32[]{:S(2)}) collective-permute-start(f32[32,64,64]{2,1,0:T(8,128)} %convolution_add_fusion.4), channel_id=1, source_target_pairs={{1,0},{2,1},{3,2},{4,3},{5,4},{6,5},{7,6},{8,7},{9,8},{10,9},{11,1... | collective-permute-start | bytes 1572872 | tf_op jit(solution)/shard_map/while/body/eval_jaxpr/ppermute | solution.py:23
  622.7 27.6 %collective-permute-start = (f32[32,64,64]{2,1,0:T(8,128)}, f32[32,64,64]{2,1,0:T(8,128)S(1)}, u32[]{:S(2)}, u32[]{:S(2)}) collective-permute-start(f32[32,64,64]{2,1,0:T(8,128)} %convolution_add_fusion.4), channel_id=1, source_target_pairs={{1,0},{2,1},{3,2},{4,3},{5,4},{6,5},{7,6},{8,7},{9,8},{10,9},{11,1... | collective-permute-start | bytes 1572872 | tf_op jit(solution)/shard_map/while/body/eval_jaxpr/ppermute | solution.py:23
  653.9 28.7 %collective-permute-start = (f32[32,64,64]{2,1,0:T(8,128)}, f32[32,64,64]{2,1,0:T(8,128)S(1)}, u32[]{:S(2)}, u32[]{:S(2)}) collective-permute-start(f32[32,64,64]{2,1,0:T(8,128)} %convolution_add_fusion.4), channel_id=1, source_target_pairs={{1,0},{2,1},{3,2},{4,3},{5,4},{6,5},{7,6},{8,7},{9,8},{10,9},{11,1... | collective-permute-start | bytes 1572872 | tf_op jit(solution)/shard_map/while/body/eval_jaxpr/ppermute | solution.py:23
  686.3 29.9 %collective-permute-start = (f32[32,64,64]{2,1,0:T(8,128)}, f32[32,64,64]{2,1,0:T(8,128)S(1)}, u32[]{:S(2)}, u32[]{:S(2)}) collective-permute-start(f32[32,64,64]{2,1,0:T(8,128)} %convolution_add_fusion.4), channel_id=1, source_target_pairs={{1,0},{2,1},{3,2},{4,3},{5,4},{6,5},{7,6},{8,7},{9,8},{10,9},{11,1... | collective-permute-start | bytes 1572872 | tf_op jit(solution)/shard_map/while/body/eval_jaxpr/ppermute | solution.py:23
  719.8 29.4 %collective-permute-start = (f32[32,64,64]{2,1,0:T(8,128)}, f32[32,64,64]{2,1,0:T(8,128)S(1)}, u32[]{:S(2)}, u32[]{:S(2)}) collective-permute-start(f32[32,64,64]{2,1,0:T(8,128)} %convolution_add_fusion.4), channel_id=1, source_target_pairs={{1,0},{2,1},{3,2},{4,3},{5,4},{6,5},{7,6},{8,7},{9,8},{10,9},{11,1... | collective-permute-start | bytes 1572872 | tf_op jit(solution)/shard_map/while/body/eval_jaxpr/ppermute | solution.py:23
  752.9 28.6 %collective-permute-start = (f32[32,64,64]{2,1,0:T(8,128)}, f32[32,64,64]{2,1,0:T(8,128)S(1)}, u32[]{:S(2)}, u32[]{:S(2)}) collective-permute-start(f32[32,64,64]{2,1,0:T(8,128)} %convolution_add_fusion.4), channel_id=1, source_target_pairs={{1,0},{2,1},{3,2},{4,3},{5,4},{6,5},{7,6},{8,7},{9,8},{10,9},{11,1... | collective-permute-start | bytes 1572872 | tf_op jit(solution)/shard_map/while/body/eval_jaxpr/ppermute | solution.py:23
  785.2 27.7 %collective-permute-start = (f32[32,64,64]{2,1,0:T(8,128)}, f32[32,64,64]{2,1,0:T(8,128)S(1)}, u32[]{:S(2)}, u32[]{:S(2)}) collective-permute-start(f32[32,64,64]{2,1,0:T(8,128)} %convolution_add_fusion.4), channel_id=1, source_target_pairs={{1,0},{2,1},{3,2},{4,3},{5,4},{6,5},{7,6},{8,7},{9,8},{10,9},{11,1... | collective-permute-start | bytes 1572872 | tf_op jit(solution)/shard_map/while/body/eval_jaxpr/ppermute | solution.py:23
  816.6 26.8 %collective-permute-start = (f32[32,64,64]{2,1,0:T(8,128)}, f32[32,64,64]{2,1,0:T(8,128)S(1)}, u32[]{:S(2)}, u32[]{:S(2)}) collective-permute-start(f32[32,64,64]{2,1,0:T(8,128)} %convolution_add_fusion.4), channel_id=1, source_target_pairs={{1,0},{2,1},{3,2},{4,3},{5,4},{6,5},{7,6},{8,7},{9,8},{10,9},{11,1... | collective-permute-start | bytes 1572872 | tf_op jit(solution)/shard_map/while/body/eval_jaxpr/ppermute | solution.py:23
  847.0 25.8 %collective-permute-start = (f32[32,64,64]{2,1,0:T(8,128)}, f32[32,64,64]{2,1,0:T(8,128)S(1)}, u32[]{:S(2)}, u32[]{:S(2)}) collective-permute-start(f32[32,64,64]{2,1,0:T(8,128)} %convolution_add_fusion.4), channel_id=1, source_target_pairs={{1,0},{2,1},{3,2},{4,3},{5,4},{6,5},{7,6},{8,7},{9,8},{10,9},{11,1... | collective-permute-start | bytes 1572872 | tf_op jit(solution)/shard_map/while/body/eval_jaxpr/ppermute | solution.py:23
  876.5 24.9 %collective-permute-start = (f32[32,64,64]{2,1,0:T(8,128)}, f32[32,64,64]{2,1,0:T(8,128)S(1)}, u32[]{:S(2)}, u32[]{:S(2)}) collective-permute-start(f32[32,64,64]{2,1,0:T(8,128)} %convolution_add_fusion.4), channel_id=1, source_target_pairs={{1,0},{2,1},{3,2},{4,3},{5,4},{6,5},{7,6},{8,7},{9,8},{10,9},{11,1... | collective-permute-start | bytes 1572872 | tf_op jit(solution)/shard_map/while/body/eval_jaxpr/ppermute | solution.py:23
  905.1 24.0 %collective-permute-start = (f32[32,64,64]{2,1,0:T(8,128)}, f32[32,64,64]{2,1,0:T(8,128)S(1)}, u32[]{:S(2)}, u32[]{:S(2)}) collective-permute-start(f32[32,64,64]{2,1,0:T(8,128)} %convolution_add_fusion.4), channel_id=1, source_target_pairs={{1,0},{2,1},{3,2},{4,3},{5,4},{6,5},{7,6},{8,7},{9,8},{10,9},{11,1... | collective-permute-start | bytes 1572872 | tf_op jit(solution)/shard_map/while/body/eval_jaxpr/ppermute | solution.py:23
  932.8 23.1 %collective-permute-start = (f32[32,64,64]{2,1,0:T(8,128)}, f32[32,64,64]{2,1,0:T(8,128)S(1)}, u32[]{:S(2)}, u32[]{:S(2)}) collective-permute-start(f32[32,64,64]{2,1,0:T(8,128)} %convolution_add_fusion.4), channel_id=1, source_target_pairs={{1,0},{2,1},{3,2},{4,3},{5,4},{6,5},{7,6},{8,7},{9,8},{10,9},{11,1... | collective-permute-start | bytes 1572872 | tf_op jit(solution)/shard_map/while/body/eval_jaxpr/ppermute | solution.py:23
  959.5 19.0 %collective-permute-start = (f32[32,64,64]{2,1,0:T(8,128)}, f32[32,64,64]{2,1,0:T(8,128)S(1)}, u32[]{:S(2)}, u32[]{:S(2)}) collective-permute-start(f32[32,64,64]{2,1,0:T(8,128)} %convolution_add_fusion.4), channel_id=1, source_target_pairs={{1,0},{2,1},{3,2},{4,3},{5,4},{6,5},{7,6},{8,7},{9,8},{10,9},{11,1... | collective-permute-start | bytes 1572872 | tf_op jit(solution)/shard_map/while/body/eval_jaxpr/ppermute | solution.py:23
  (46 other events, 104.0 us)
where the time goes:
time: 1040 us; the launch traced here: 1030 us
  waiting for transfers between devices  578 us (56%)
  starting transfers between devices  199 us (19%)
  matrix products  177 us (17%)
  local copies, waits for them, and re-layouts  66.4 us (6%)
    ppermute x31, waiting for transfers between devices, shifted(): lax.ppermute(value, axis, [(source, source + steps) for source in range(i...  578 us
    ppermute x31, starting transfers between devices, shifted(): lax.ppermute(value, axis, [(source, source + steps) for source in range(i...  199 us
    dot_general x31, matrix products, advance(): shard_begin = inner_product('hde,hef->hdf', linear, adjoint_end) + offset  114 us
  transfers between devices with their start and end apart: 32, of which 31 were waited for; matrix products, arithmetic and copies ran while one was open for 3% of the time, Pallas kernels for 0%

commit v1 on v0

v1 whole, which is shorter than its diff:
```python
from functools import partial

import jax
import jax.numpy as jnp
from jax import lax
from jax.experimental import pallas as pl
from jax.experimental.pallas import tpu as pltpu
from jax.sharding import PartitionSpec as P

DH = 64
QUAD = 4 * DH
PAIRS = QUAD // 128
HEADS = QUAD // DH
F32 = jnp.float32
BF16 = jnp.bfloat16
CHUNKS = 4
CODE_SPAN = 250.0
CODE_BASE = -125.0


def quad_iota():
    row = lax.broadcasted_iota(jnp.int32, (DH, QUAD), 0)
    lane = lax.broadcasted_iota(jnp.int32, (DH, QUAD), 1)
    return row, lane % DH, lane // DH


def head_masks():
    head = quad_iota()[2]
    return [(head == h).astype(F32).astype(BF16) for h in range(QUAD // DH)]


def diagonal(right, masks):
    return jnp.concatenate([right * mask for mask in masks], axis=0)


def times(left, block):
    return lax.dot_general(left, block, (((1,), (0,)), ((), ())), preferred_element_type=F32)


def times_t(left, block):
    return lax.dot_general(left, block, (((1,), (1,)), ((), ())), preferred_element_type=F32)


def split(value):
    high = value.astype(BF16)
    low = (value - high.astype(F32)).astype(BF16)
    return high, low


def both(high, low):
    return jnp.concatenate([high, low], axis=0)


def folded(product):
    return product[:DH] + product[DH:]


def column_scale(value):
    largest = jnp.max(jnp.abs(value), axis=0, keepdims=True)
    return (jnp.maximum(largest, 1e-30) * 1.01).astype(BF16).astype(F32)


def encode(value, scale):
    size = jnp.exp2(jnp.abs(value) * (CODE_SPAN / scale) + CODE_BASE)
    return jnp.where(value < 0, -size, size)


def decode(code, scale):
    size = (jnp.log2(jnp.abs(code)) - CODE_BASE) * (scale / CODE_SPAN)
    return jnp.where(code < 0, -size, size)


def chunk(ref, i, features):
    if ref.shape[1] != features:
        size = ref.shape[0] // CHUNKS
        return ref.at[pl.ds(pl.multiple_of(i * size, size), size), :]
    size = features // CHUNKS
    return ref.at[:, pl.ds(pl.multiple_of(i * size, size), size)]


def rates(rate_ref, index):
    head = lax.broadcasted_iota(jnp.int32, (DH, QUAD), 1) // DH
    value = jnp.full((DH, QUAD), rate_ref[0, index * HEADS], F32)
    for h in range(1, HEADS):
        value = jnp.where(head == h, rate_ref[0, index * HEADS + h], value)
    return value * (1.0 / DH)


def mover(sources, targets, sems, features):
    def copies(i):
        return [
            pltpu.make_async_copy(chunk(source, i, features), chunk(target, i, features), sems.at[n, i])
            for n, (source, target) in enumerate(zip(sources, targets))
        ]

    def start(i):
        for copy in copies(i):
            copy.start()

    def wait(i):
        for copy in copies(i):
            copy.wait()

    return start, wait


def run(work, count, fetch=None, ship=None):
    each = count // CHUNKS
    if fetch is not None:
        fetch[0](0)
        fetch[0](1)

    def body(i, carry):
        if fetch is not None:
            fetch[1](i)

            @pl.when(i + 2 < CHUNKS)
            def _():
                fetch[0](i + 2)

        for t in range(each):
            index = i * each + t
            work(index, pl.ds(pl.multiple_of(index * QUAD, QUAD), QUAD), t)
        if ship is not None:
            ship[0](i)
        return carry

    lax.fori_loop(0, CHUNKS, body, 0)
    if ship is not None:
        for i in range(CHUNKS):
            ship[1](i)


def map_kernel(q_hbm, k_hbm, rate_ref, acode_ref, ascale_ref, mt_ref, q_ref, k_ref, in_sems):
    row, col, _ = quad_iota()
    masks = head_masks()
    identity = (row == col).astype(F32).astype(BF16)
    upper = (row <= col).astype(F32)

    def work(index, lanes, t):
        rate = rates(rate_ref, index)
        gates, readouts = [], []
        for b in range(2):
            rows = slice(b * DH, (b + 1) * DH)
            k, q = k_ref[rows, lanes], q_ref[rows, lanes]
            k_block, q_block = diagonal(k, masks), diagonal(q, masks)
            on_q = times_t(both(k, identity), q_block)
            st_hi, st_lo = split(on_q[:DH] * upper)
            qt = on_q[DH:]
            kt = times_t(identity, k_block).astype(BF16)
            gates.append(rate * times(kt, k_block))
            readouts.append(qt - rate * (times(kt, diagonal(st_hi, masks)) + times(kt, diagonal(st_lo, masks))))
        g_hi, g_lo = split(gates[0])
        g_both = both(g_hi, g_lo)

        def gate_times(value):
            hi, lo = split(value)
            return folded(times(g_both, diagonal(hi, masks))) + times(g_hi, diagonal(lo, masks))

        drop = gates[0] + gates[1] - gate_times(gates[1])
        second = readouts[1] - gate_times(readouts[1])
        for b, value in enumerate((readouts[0], second)):
            hi, lo = split(value)
            mt_ref[b * 128 : b * 128 + 64, lanes] = hi
            mt_ref[b * 128 + 64 : b * 128 + 128, lanes] = lo
        scale = column_scale(drop)
        acode_ref[:, lanes] = encode(drop, scale).astype(BF16)
        ascale_ref[:, lanes] = jnp.broadcast_to(scale, (8, QUAD))

    features = k_ref.shape[1]
    run(work, features // QUAD, mover((q_hbm, k_hbm), (q_ref, k_ref), in_sems, features))


def pack_kernel(mt_ref, dz_ref, acode_ref, ascale_ref, out_ref):
    masks = head_masks()
    left = lax.broadcasted_iota(jnp.int32, (DH, 128), 1) < DH
    left8 = left[:8]

    def work(index, lanes, t):
        total = folded(times(mt_ref[0:128, lanes], diagonal(dz_ref[0:DH, lanes], masks)))
        total += folded(times(mt_ref[128:256, lanes], diagonal(dz_ref[DH:128, lanes], masks)))
        scale = column_scale(total)
        code = encode(total, scale)
        a_code = acode_ref[:, lanes].astype(F32)
        a_scale = ascale_ref[:, lanes]
        scale = jnp.broadcast_to(scale, (8, QUAD))
        for p in range(PAIRS):
            cut = slice(p * 128, p * 128 + 128)
            head = index * HEADS + p * 2
            out_ref[head, 0:DH, :] = jnp.where(left, a_code[:, cut], pltpu.roll(code[:, cut], DH, 1)).astype(BF16)
            out_ref[head, DH : DH + 8, :] = jnp.where(left8, a_scale[:, cut], pltpu.roll(scale[:, cut], DH, 1)).astype(BF16)
            out_ref[head + 1, 0:DH, :] = jnp.where(left, pltpu.roll(a_code[:, cut], DH, 1), code[:, cut]).astype(BF16)
            out_ref[head + 1, DH : DH + 8, :] = jnp.where(left8, pltpu.roll(a_scale[:, cut], DH, 1), scale[:, cut]).astype(BF16)

    run(work, dz_ref.shape[1] // QUAD)


def relay_kernel(in_ref, out_ref, map_ref, left_ref, group):
    shards = in_ref.shape[0]
    row = lax.broadcasted_iota(jnp.int32, (DH, 128), 0)
    lane = lax.broadcasted_iota(jnp.int32, (DH, 128), 1)
    left = lane < DH
    unit = (row == lane).astype(F32)

    def unpack(j, carry):
        scale = in_ref[j, DH : DH + 8, :].astype(F32)[0:1]
        value = decode(in_ref[j, 0:DH, :].astype(F32), scale)
        value = jnp.where(left, unit - value, value)
        map_ref[j] = value
        left_ref[j] = left_operand(value)
        return carry

    def left_operand(value):
        hi, lo = split(value)
        hi_f = hi.astype(F32)
        lo_f = lo.astype(F32)
        first = jnp.where(left, hi_f, pltpu.roll(lo_f, DH, 1)).astype(BF16)
        last = jnp.where(left, hi_f, 0.0).astype(BF16)
        return jnp.concatenate([first, last], axis=1)

    def right_operand(value):
        hi, lo = split(value)
        return jnp.concatenate([hi, hi, lo, jnp.zeros_like(lo)], axis=0)

    lax.fori_loop(0, shards, unpack, 0, unroll=4)
    groups = shards // group
    suffix = [map_ref[g * group + group - 1] for g in range(groups)]
    for step in range(group - 2, -1, -1):
        for g in range(groups):
            j = g * group + step
            own = map_ref[j]
            suffix[g] = times(left_ref[j], right_operand(suffix[g])) + jnp.where(left, 0.0, own)
            map_ref[j] = suffix[g]
            left_ref[j] = left_operand(suffix[g])
    ends = [None] * groups
    ends[groups - 1] = jnp.zeros((DH, 128), F32)
    for g in range(groups - 2, -1, -1):
        j = (g + 1) * group
        ends[g] = times(left_ref[j], right_operand(ends[g + 1])) + map_ref[j]
    for g in range(groups):
        right = right_operand(ends[g])
        found = []
        for step in range(group):
            j = g * group + step
            if step == group - 1:
                found.append(ends[g])
            else:
                found.append(times(left_ref[j + 1], right) + map_ref[j + 1])
        for step in range(0, group, 2):
            pair = jnp.where(left, pltpu.roll(found[step], DH, 1), found[step + 1])
            scale = column_scale(pair)
            code = encode(pair, scale)
            turned = pltpu.roll(code, DH, 1)
            scale = jnp.broadcast_to(scale, (8, 128))
            j = g * group + step
            half = DH // 2
            low = left[:half]
            out_ref[j, 0:half, :] = jnp.where(low, code[:half], turned[half:]).astype(BF16)
            other = pltpu.roll(scale, DH, 1)
            out_ref[j, half : half + 8, :] = jnp.where(left[:8], scale, other).astype(BF16)
            out_ref[j + 1, 0:half, :] = jnp.where(low, turned[:half], code[half:]).astype(BF16)
            out_ref[j + 1, half : half + 8, :] = jnp.where(left[:8], other, scale).astype(BF16)


def trail_kernel(rate_ref, *refs):
    inputs, outputs, (flat_ref, in_sems, out_sems) = refs[:5], refs[5:10], refs[20:]
    q_ref, k_ref, v_ref, w_ref, dz_ref = refs[10:15]
    e_ref, wt_ref, kt_ref, t_ref, outer_ref = refs[15:20]
    row, col, _ = quad_iota()
    masks = head_masks()
    identity = (row == col).astype(F32).astype(BF16)
    upper = (row <= col).astype(F32)
    half = DH // 2
    low = lax.broadcasted_iota(jnp.int32, (half, 128), 1) < DH

    def start_weight(pair):
        first = pl.multiple_of(pair * DH, DH)
        one = flat_ref[pl.ds(first, half), :]
        two = flat_ref[pl.ds(first + half, half), :]
        even = jnp.where(low, one, pltpu.roll(two, DH, 1))
        odd = jnp.where(low, pltpu.roll(one, DH, 1), two)
        flat_ref[pl.ds(first, half, stride=2), :] = even
        flat_ref[pl.ds(first + 1, half, stride=2), :] = odd
        return flat_ref[pl.ds(first, DH), :]

    def work(index, lanes, t):
        rate = rates(rate_ref, index)
        if t == 0:
            first = pl.multiple_of(index * HEADS, 8)
            for i in range(half):
                flat_ref[pl.ds(first * half + i, 8, stride=half), :] = w_ref[pl.ds(first, 8), i * 128 : (i + 1) * 128]
        weight = jnp.concatenate([start_weight(index * PAIRS + p) for p in range(PAIRS)], axis=1)
        for b in range(2):
            rows = slice(b * DH, (b + 1) * DH)
            hi_rows, lo_rows = slice(b * 128, b * 128 + 64), slice(b * 128 + 64, b * 128 + 128)
            k = k_ref[rows, lanes]
            w_hi, w_lo = split(weight)
            wt_ref[hi_rows, lanes] = w_hi
            wt_ref[lo_rows, lanes] = w_lo
            error = times(k, diagonal(w_hi, masks)) + times(k, diagonal(w_lo, masks)) - v_ref[rows, lanes].astype(F32)
            e_hi, e_lo = split(error)
            e_ref[hi_rows, lanes] = e_hi
            e_ref[lo_rows, lanes] = e_lo
            kt = times_t(identity, diagonal(k, masks)).astype(BF16)
            kt_ref[rows, lanes] = kt
            if b == 0:
                weight = weight - rate * (times(kt, diagonal(e_hi, masks)) + times(kt, diagonal(e_lo, masks)))
            on_q = times_t(both(k, identity), diagonal(q_ref[rows, lanes], masks))
            st_hi, st_lo = split(on_q[:DH] * upper)
            qt = on_q[DH:].astype(BF16)
            on_dz = times(jnp.concatenate([st_hi, st_lo, qt], axis=0), diagonal(dz_ref[rows, lanes], masks))
            t_ref[rows, lanes] = on_dz[:DH] + on_dz[DH:128]
            outer_ref[rows, lanes] = on_dz[128:]

    features = k_ref.shape[1]
    fetch = mover(inputs, refs[10:15], in_sems, features)
    ship = mover(refs[15:20], outputs, out_sems, features)
    run(work, features // QUAD, fetch, ship)


def direct_kernel(rate_ref, *refs):
    inputs, outputs, (in_sems, out_sems) = refs[:5], refs[5:7], refs[14:]
    q_ref, k_ref, dz_ref, e_ref, wt_ref = refs[7:12]
    gq_ref, part_ref = refs[12:14]
    row, col, _ = quad_iota()
    masks = head_masks()
    upper = (row <= col).astype(F32)
    lower = (row >= col).astype(F32)

    def work(index, lanes, t):
        rate = rates(rate_ref, index)
        for b in range(2):
            rows = slice(b * DH, (b + 1) * DH)
            two = slice(b * 128, b * 128 + 128)
            hi_rows, lo_rows = slice(b * 128, b * 128 + 64), slice(b * 128 + 64, b * 128 + 128)
            dz = dz_ref[rows, lanes]
            dpt = folded(times_t(e_ref[two, lanes], diagonal(dz, masks))) * (-rate * upper)
            dp = times_t(dz, diagonal(e_ref[hi_rows, lanes], masks)) + times_t(dz, diagonal(e_ref[lo_rows, lanes], masks))
            dp = dp * (-rate * lower)
            grad = times_t(dz, diagonal(wt_ref[hi_rows, lanes], masks)) + times_t(dz, diagonal(wt_ref[lo_rows, lanes], masks))
            grad += folded(times(both(*split(dp)), diagonal(k_ref[rows, lanes], masks)))
            gq_ref[rows, lanes] = grad.astype(BF16)
            part_ref[rows, lanes] = folded(times(both(*split(dpt)), diagonal(q_ref[rows, lanes], masks)))

    features = k_ref.shape[1]
    run(work, features // QUAD, mover(inputs, refs[7:12], in_sems, features), mover(refs[12:14], outputs, out_sems, features))


def final_kernel(rate_ref, code_hbm, *refs):
    inputs, outputs = refs[:7], refs[7:10]
    k_ref, kt_ref, e_ref, wt_ref, t_ref, outer_ref, part_ref = refs[10:17]
    gk_ref, gv_ref, start_ref, code_ref, flat_ref, in_sems, out_sems, code_sems = refs[17:]

    def code_copy(i):
        size = code_ref.shape[0] // CHUNKS
        part = pl.ds(i * size, size)
        return pltpu.make_async_copy(code_hbm.at[part], code_ref.at[part], code_sems.at[i])

    masks = head_masks()
    half = DH // 2
    low = lax.broadcasted_iota(jnp.int32, (half, 128), 1) < DH

    def work(index, lanes, t):
        rate = rates(rate_ref, index)
        pairs = []
        for p in range(PAIRS):
            halves = []
            for h in range(2):
                head = index * HEADS + p * 2 + h
                scale = code_ref[head, half : half + 8, :].astype(F32)[0:1]
                halves.append(decode(code_ref[head, 0:half, :].astype(F32), scale))
            top = jnp.where(low, halves[0], pltpu.roll(halves[1], DH, 1))
            bottom = jnp.where(low, pltpu.roll(halves[0], DH, 1), halves[1])
            pairs.append(jnp.concatenate([top, bottom], axis=0))
        adjoint = jnp.concatenate(pairs, axis=1)
        for b in (1, 0):
            rows = slice(b * DH, (b + 1) * DH)
            two = slice(b * 128, b * 128 + 128)
            hi_rows, lo_rows = slice(b * 128, b * 128 + 64), slice(b * 128 + 64, b * 128 + 128)
            g_hi, g_lo = split(adjoint)
            g_block, g_low_block = diagonal(g_hi, masks), diagonal(g_lo, masks)
            k = k_ref[rows, lanes]
            slope = t_ref[rows, lanes] + times(k, g_block) + times(k, g_low_block)
            grad_error = -rate * slope
            gv_ref[rows, lanes] = (-grad_error).astype(BF16)
            d_hi, d_lo = split(grad_error)
            kt = kt_ref[rows, lanes]
            grad = part_ref[rows, lanes]
            grad += folded(times_t(both(d_hi, d_lo), diagonal(wt_ref[hi_rows, lanes], masks)))
            grad += times_t(d_hi, diagonal(wt_ref[lo_rows, lanes], masks))
            on_g = folded(times_t(e_ref[two, lanes], g_block)) + times_t(e_ref[hi_rows, lanes], g_low_block)
            gk_ref[rows, lanes] = (grad - rate * on_g).astype(BF16)
            adjoint = adjoint + outer_ref[rows, lanes] + times(kt, diagonal(d_hi, masks)) + times(kt, diagonal(d_lo, masks))
        for p in range(PAIRS):
            first = pl.multiple_of((index * PAIRS + p) * DH, DH)
            flat_ref[pl.ds(first, DH), :] = adjoint[:, p * 128 : p * 128 + 128]
            even = flat_ref[pl.ds(first, half, stride=2), :]
            odd = flat_ref[pl.ds(first + 1, half, stride=2), :]
            flat_ref[pl.ds(first, half), :] = jnp.where(low, even, pltpu.roll(odd, DH, 1))
            flat_ref[pl.ds(first + half, half), :] = jnp.where(low, pltpu.roll(even, DH, 1), odd)
        if (t + 1) * HEADS == 8:
            head = pl.multiple_of((index + 1) * HEADS - 8, 8)
            for i in range(half):
                start_ref[pl.ds(head, 8), i * 128 : (i + 1) * 128] = flat_ref[pl.ds(head * half + i, 8, stride=half), :]

    features = k_ref.shape[1]
    start, wait = mover(inputs, refs[10:17], in_sems, features)

    def start_all(i):
        code_copy(i).start()
        start(i)

    def wait_all(i):
        code_copy(i).wait()
        wait(i)

    run(work, features // QUAD, (start_all, wait_all), mover((gk_ref, gv_ref, start_ref), outputs, out_sems, features))


def call(kernel, ins, outs, flops, scratch=(), limit=58):
    args = [array for array, _ in ins]
    size = sum(a.size * a.dtype.itemsize for a in args) + sum(o.size * o.dtype.itemsize for o, _ in outs)
    return pl.pallas_call(
        kernel,
        out_shape=tuple(shape for shape, _ in outs),
        in_specs=[pl.BlockSpec(memory_space=memory) for _, memory in ins],
        out_specs=tuple(pl.BlockSpec(memory_space=memory) for _, memory in outs),
        scratch_shapes=list(scratch),
        compiler_params=pltpu.CompilerParams(vmem_limit_bytes=limit * 1024 * 1024),
        cost_estimate=pl.CostEstimate(flops=flops, bytes_accessed=size, transcendentals=0),
    )(*args)


def per_device(queries, memory_keys, memory_values, upstream, inner_rate, checkpoints):
    sections = lax.axis_size("section")
    shards = lax.axis_size("seq")
    heads = inner_rate.shape[1]
    features = queries.shape[2]
    tokens = queries.shape[1]
    q, k, v, w = queries[0], memory_keys[0], memory_values[0], checkpoints[0, 0]

    def array(rows, kind, columns=features):
        return jax.ShapeDtypeStruct((rows, columns), kind)

    def apart(a):
        return jax.ShapeDtypeStruct((a.shape[0] * CHUNKS, a.shape[1] // CHUNKS), a.dtype)

    def buffers(arrays):
        return [pltpu.VMEM(a.shape, a.dtype) for a in arrays]

    def semaphores(count):
        return pltpu.SemaphoreType.DMA((count, CHUNKS))

    def outside(arrays):
        return [(a, pltpu.HBM) for a in arrays]

    def inside(arrays):
        return [(a, pltpu.VMEM) for a in arrays]

    rate = [(inner_rate, pltpu.SMEM)]
    unit = 2 * tokens * features * QUAD
    flat = pltpu.VMEM((heads * DH // 2, 128), F32)
    single, whole, double = array(tokens, F32), array(tokens, BF16), array(2 * tokens, BF16)

    cotangent = lax.ppermute(upstream, "section", [((i + 1) % sections, i) for i in range(sections)])
    dz = cotangent[0]
    acode, ascale, mt = call(
        map_kernel,
        outside([q, k]) + rate,
        inside([array(DH, BF16), array(8, F32), double]),
        8 * unit,
        buffers([q, k]) + [semaphores(2)],
        24,
    )
    (packed,) = call(
        pack_kernel, inside([mt, dz, acode, ascale]), inside([jax.ShapeDtypeStruct((heads, DH + 8, 128), BF16)]), 2 * unit, (), 24
    )
    arrived = lax.all_to_all(packed, "seq", 0, 0, tiled=True)
    rate_later, _ = lax.optimization_barrier((inner_rate, packed))
    given, made = [q, k, v, w, dz], [double, double, whole, single, single]
    error, weights, kt, slope, outer = call(
        trail_kernel,
        [(rate_later, pltpu.SMEM)] + outside(given),
        outside([apart(a) for a in made]),
        10 * unit,
        buffers(given + made) + [flat, semaphores(5), semaphores(5)],
    )
    arrived, slope = lax.optimization_barrier((arrived, slope))
    (ends,) = call(
        partial(relay_kernel, group=8),
        inside([arrived]),
        inside([jax.ShapeDtypeStruct((shards, DH // 2 + 8, 128), BF16)]),
        unit,
        [pltpu.VMEM((shards, DH, 128), F32), pltpu.VMEM((shards, DH, 256), BF16)],
        24,
    )
    returned = lax.all_to_all(ends, "seq", 0, 0, tiled=True)
    rate_later, _ = lax.optimization_barrier((inner_rate, ends))
    given, held, made = [q, k, dz, error, weights], [whole, whole, whole, double, double], [whole, single]
    grad_q, part = call(
        direct_kernel,
        [(rate_later, pltpu.SMEM)] + outside(given),
        outside([whole, apart(single)]),
        10 * unit,
        buffers(held + made) + [semaphores(5), semaphores(2)],
    )
    given, held = [k, kt, error, weights, slope, outer, part], [whole, whole, double, double, single, single, single]
    made = [whole, whole, array(heads, F32, DH * DH)]
    grad_k, grad_v, start = call(
        final_kernel,
        rate + outside([returned] + given),
        outside(made),
        10 * unit,
        buffers(held + made + [returned]) + [flat, semaphores(7), semaphores(3), pltpu.SemaphoreType.DMA((CHUNKS,))],
    )
    return grad_q[None], grad_k[None], grad_v[None], start[None, None]


def solution(mesh):
    tokens = P("section", "seq", None)
    return jax.shard_map(
        per_device,
        mesh=mesh,
        in_specs=(tokens, tokens, tokens, tokens, P("section", None), P("section", "seq", None, None)),
        out_specs=(tokens, tokens, tokens, P("section", "seq", None, None)),
        check_vma=False,
    )
```

time: 1040 us -> 78.6 us (0.08)
  the two profiles are of different devices: /device:TPU:22 before, /device:TPU:40 now
where the time goes in v1:
time: 78.6 us; the launch traced here: 78 us
  Pallas kernels  42.5 us (54%)
  starting transfers between devices  16.2 us (21%)
  waiting for transfers between devices  15.1 us (19%)
  local copies, waits for them, and re-layouts  3.48 us (4%)
    pallas_call x6, Pallas kernels, call(): pl.pallas_call(kernel, out_shape=tuple((shape for shape, _ in outs)), in_...  42.5 us
    all_to_all x1, starting transfers between devices, per_device(): arrived = lax.all_to_all(packed, 'seq', 0, 0, tiled=True)  11.2 us
    all_to_all x1, waiting for transfers between devices, per_device(): arrived = lax.all_to_all(packed, 'seq', 0, 0, tiled=True)  9.84 us
    all_to_all x1, waiting for transfers between devices, per_device(): returned = lax.all_to_all(ends, 'seq', 0, 0, tiled=True)  5.27 us
    all_to_all x1, starting transfers between devices, per_device(): returned = lax.all_to_all(ends, 'seq', 0, 0, tiled=True)  5.01 us
    unnamed x10, local copies, waits for them, and re-layouts  3.48 us
  transfers between devices with their start and end apart: 3, of which 2 were waited for; matrix products, arithmetic and copies ran while one was open for 0% of the time, Pallas kernels for 32%

profile of v1, /device:TPU:40, one launch (start us, length us, event | category | flops | bytes accessed | tf_op | source)
XLA Modules:
  0.0 78.0 jit_solution(4331003762565810920)
XLA Ops:
  0.6 0.0 collective-permute-start
  0.7 0.0 copy-start.2
  0.7 0.6 copy-done.2
  1.3 0.0 copy-start.1
  1.3 1.0 %copy-done.1 = bf16[1,128,2048]{2,1,0:T(8,128)(2,1)S(1)} copy-done((bf16[1,128,2048]{2,1,0:T(8,128)(2,1)S(1)}, bf16[1,128,2048]{2,1,0:T(8,128)(2,1)}, u32[]{:S(2)}) %copy-start.1) | copy-done | bytes 524312
  2.4 0.0 copy-start.3
  2.4 1.0 %copy-done.3 = bf16[1,128,2048]{2,1,0:T(8,128)(2,1)S(1)} copy-done((bf16[1,128,2048]{2,1,0:T(8,128)(2,1)S(1)}, bf16[1,128,2048]{2,1,0:T(8,128)(2,1)}, u32[]{:S(2)}) %copy-start.3) | copy-done | bytes 524312
  3.4 7.3 %shard_map.93 = (bf16[64,2048]{1,0:T(8,128)(2,1)S(1)}, f32[8,2048]{1,0:T(8,128)S(1)}, bf16[256,2048]{1,0:T(8,128)(2,1)S(1)}) custom-call(bf16[128,2048]{1,0:T(8,128)(2,1)S(1)} %bitcast.18, bf16[128,2048]{1,0:T(8,128)(2,1)S(1)} %bitcast.15, f32[1,32]{1,0:T(1,128)S(1)} %copy-done.2), custom_call_target="tpu_custom_call" | custom-call | flops 1073741824 | bytes 2424960 | tf_op jit(solution)/shard_map/pallas_call | solution.py:423
  10.7 0.0 collective-permute-done
  10.7 0.0 copy-start
  10.7 2.4 %shard_map.94 = bf16[32,72,128]{2,1,0:T(8,128)(2,1)} custom-call(bf16[256,2048]{1,0:T(8,128)(2,1)S(1)} %get-tuple-element.21.mt_ref, bf16[128,2048]{1,0:T(8,128)(2,1)S(1)} %bitcast.9, bf16[64,2048]{1,0:T(8,128)(2,1)S(1)} %get-tuple-element.22.acode_ref, f32[8,2048]{1,0:T(8,128)S(1)} %get-tuple-element.23.ascale_ref), custom_call_target="tpu_custom_call" | custom-call | flops 268435456 | bytes 2490368 | tf_op jit(solution)/shard_map/pallas_call | solution.py:423
  13.1 0.0 copy-done
  13.1 11.2 %all-to-all-start = ((bf16[32,72,128]{2,1,0:T(8,128)(2,1)}), bf16[32,72,128]{2,1,0:T(8,128)(2,1)S(1)}, u32[]{:S(2)}, u32[]{:S(2)}) async-start(bf16[32,72,128]{2,1,0:T(8,128)(2,1)} %shard_map.94), calls=%async_computation | async-start | bytes 1179648 | tf_op jit(solution)/shard_map/all_to_all | solution.py:478
  24.3 9.7 %shard_map.95 = (bf16[1024,512]{1,0:T(8,128)(2,1)}, bf16[1024,512]{1,0:T(8,128)(2,1)}, bf16[512,512]{1,0:T(8,128)(2,1)}, f32[512,512]{1,0:T(8,128)}, f32[512,512]{1,0:T(8,128)}) custom-call(f32[1,32]{1,0:T(1,128)} %rate_ref.5, bf16[128,2048]{1,0:T(8,128)(2,1)} %bitcast.16, bf16[128,2048]{1,0:T(8,128)(2,1)} %bitcast.12, bf16[128,2048]{1,0:T(8,128)(2,1)} %bitcast.19, ...), custom_call_target="tpu_custom_call" | custom-call | flops 1342177280 | bytes 7340160 | tf_op jit(solution)/shard_map/pallas_call | solution.py:423
  34.0 9.8 %all-to-all-done.in_ref = bf16[32,72,128]{2,1,0:T(8,128)(2,1)S(1)} async-done(((bf16[32,72,128]{2,1,0:T(8,128)(2,1)}), bf16[32,72,128]{2,1,0:T(8,128)(2,1)S(1)}, u32[]{:S(2)}, u32[]{:S(2)}) %all-to-all-start) | async-done | bytes 589856 | tf_op jit(solution)/shard_map/all_to_all | solution.py:478
  43.8 4.2 %shard_map.96 = bf16[32,40,128]{2,1,0:T(8,128)(2,1)} custom-call(bf16[32,72,128]{2,1,0:T(8,128)(2,1)S(1)} %all-to-all-done.in_ref), custom_call_target="tpu_custom_call" | custom-call | flops 134217728 | bytes 917504 | tf_op jit(solution)/shard_map/pallas_call | solution.py:423
  48.1 5.0 %all-to-all-start.1 = ((bf16[32,40,128]{2,1,0:T(8,128)(2,1)}), bf16[32,40,128]{2,1,0:T(8,128)(2,1)S(1)}, u32[]{:S(2)}, u32[]{:S(2)}) async-start(bf16[32,40,128]{2,1,0:T(8,128)(2,1)} %shard_map.96), calls=%async_computation.1 | async-start | bytes 655360 | tf_op jit(solution)/shard_map/all_to_all | solution.py:497
  53.1 7.9 %shard_map.97 = (bf16[128,2048]{1,0:T(8,128)(2,1)}, f32[512,512]{1,0:T(8,128)}) custom-call(f32[1,32]{1,0:T(1,128)} %rate_ref.5, bf16[128,2048]{1,0:T(8,128)(2,1)} %bitcast.17, bf16[128,2048]{1,0:T(8,128)(2,1)} %bitcast.13, bf16[128,2048]{1,0:T(8,128)(2,1)} %bitcast.11, bf16[1024,512]{1,0:T(8,128)(2,1)} %get-tuple-element.28.refs_3_.refs_2_, ...), custom_call_target="tpu_custom_call" | custom-call | flops 1342177280 | bytes 5243008 | tf_op jit(solution)/shard_map/pallas_call | solution.py:423
  61.1 5.3 %all-to-all-done.1.code_hbm = bf16[32,40,128]{2,1,0:T(8,128)(2,1)S(1)} async-done(((bf16[32,40,128]{2,1,0:T(8,128)(2,1)}), bf16[32,40,128]{2,1,0:T(8,128)(2,1)S(1)}, u32[]{:S(2)}, u32[]{:S(2)}) %all-to-all-start.1) | async-done | bytes 327712 | tf_op jit(solution)/shard_map/all_to_all | solution.py:497
  66.3 0.0 copy-start.4
  66.3 0.7 copy-done.4
  67.1 11.0 %shard_map.98 = (bf16[128,2048]{1,0:T(8,128)(2,1)}, bf16[128,2048]{1,0:T(8,128)(2,1)}, f32[32,4096]{1,0:T(8,128)}) custom-call(f32[1,32]{1,0:T(1,128)} %rate_ref.5, bf16[32,40,128]{2,1,0:T(8,128)(2,1)} %copy-done.4, bf16[128,2048]{1,0:T(8,128)(2,1)} %bitcast.14, bf16[512,512]{1,0:T(8,128)(2,1)} %get-tuple-element.31.refs_1_, ...), custom_call_target="tpu_custom_call" | custom-call | flops 1342177280 | bytes 8192128 | tf_op jit(solution)/shard_map/pallas_call | solution.py:423
Async XLA Ops:
  0.6 10.1 %collective-permute-start = (bf16[1,128,2048]{2,1,0:T(8,128)(2,1)}, bf16[1,128,2048]{2,1,0:T(8,128)(2,1)S(1)}, u32[]{:S(2)}, u32[]{:S(2)}) collective-permute-start(bf16[1,128,2048]{2,1,0:T(8,128)(2,1)} %param.9), channel_id=1, source_target_pairs={{32,0},{64,32},{96,64},{128,96},{160,128},{192,160},{224,192},{0,2... | collective-permute-start | bytes 1572872 | tf_op jit(solution)/shard_map/ppermute | solution.py:465
  0.7 0.7 copy-start.2
  1.3 1.0 %copy-start.1 = (bf16[1,128,2048]{2,1,0:T(8,128)(2,1)S(1)}, bf16[1,128,2048]{2,1,0:T(8,128)(2,1)}, u32[]{:S(2)}) copy-start(bf16[1,128,2048]{2,1,0:T(8,128)(2,1)} %param.7) | copy-start | bytes 1572868
  2.4 1.0 %copy-start.3 = (bf16[1,128,2048]{2,1,0:T(8,128)(2,1)S(1)}, bf16[1,128,2048]{2,1,0:T(8,128)(2,1)}, u32[]{:S(2)}) copy-start(bf16[1,128,2048]{2,1,0:T(8,128)(2,1)} %param.6) | copy-start | bytes 1572868
  10.7 2.4 %copy-start = (bf16[1,128,2048]{2,1,0:T(8,128)(2,1)}, bf16[1,128,2048]{2,1,0:T(8,128)(2,1)S(1)}, u32[]{:S(2)}) copy-start(bf16[1,128,2048]{2,1,0:T(8,128)(2,1)S(1)} %collective-permute-done) | copy-start | bytes 1572868
  13.1 30.7 %all-to-all-start = ((bf16[32,72,128]{2,1,0:T(8,128)(2,1)}), bf16[32,72,128]{2,1,0:T(8,128)(2,1)S(1)}, u32[]{:S(2)}, u32[]{:S(2)}) async-start(bf16[32,72,128]{2,1,0:T(8,128)(2,1)} %shard_map.94), calls=%async_computation | async-start | bytes 1179648 | tf_op jit(solution)/shard_map/all_to_all | solution.py:478
  48.1 18.2 %all-to-all-start.1 = ((bf16[32,40,128]{2,1,0:T(8,128)(2,1)}), bf16[32,40,128]{2,1,0:T(8,128)(2,1)S(1)}, u32[]{:S(2)}, u32[]{:S(2)}) async-start(bf16[32,40,128]{2,1,0:T(8,128)(2,1)} %shard_map.96), calls=%async_computation.1 | async-start | bytes 655360 | tf_op jit(solution)/shard_map/all_to_all | solution.py:497
  66.3 0.7 copy-start.4

commit v2 on v1

--- a/solution.py
+++ b/solution.py
@@ -14,6 +14,8 @@
 F32 = jnp.float32
 BF16 = jnp.bfloat16
 CHUNKS = 4
+MAP_LIMIT = 24
+LATE_LIMIT = 24
 CODE_SPAN = 250.0
 CODE_BASE = -125.0
 
@@ -104,19 +106,19 @@
     return start, wait
 
 
-def run(work, count, fetch=None, ship=None):
+def run(work, count, fetch, ship=None, first=None):
     each = count // CHUNKS
-    if fetch is not None:
-        fetch[0](0)
-        fetch[0](1)
+    first.start()
+    fetch[0](0)
+    fetch[0](1)
+    first.wait()
 
     def body(i, carry):
-        if fetch is not None:
-            fetch[1](i)
-
-            @pl.when(i + 2 < CHUNKS)
-            def _():
-                fetch[0](i + 2)
+        fetch[1](i)
+
+        @pl.when(i + 2 < CHUNKS)
+        def _():
+            fetch[0](i + 2)
 
         for t in range(each):
             index = i * each + t
@@ -131,7 +133,7 @@
             ship[1](i)
 
 
-def map_kernel(q_hbm, k_hbm, rate_ref, acode_ref, ascale_ref, mt_ref, q_ref, k_ref, in_sems):
+def map_kernel(rate_hbm, q_hbm, k_hbm, acode_ref, ascale_ref, mt_ref, rate_ref, rate_sem, q_ref, k_ref, in_sems):
     row, col, _ = quad_iota()
     masks = head_masks()
     identity = (row == col).astype(F32).astype(BF16)
@@ -168,7 +170,8 @@
         ascale_ref[:, lanes] = jnp.broadcast_to(scale, (8, QUAD))
 
     features = k_ref.shape[1]
-    run(work, features // QUAD, mover((q_hbm, k_hbm), (q_ref, k_ref), in_sems, features))
+    fetch = mover((q_hbm, k_hbm), (q_ref, k_ref), in_sems, features)
+    run(work, features // QUAD, fetch, None, pltpu.make_async_copy(rate_hbm, rate_ref, rate_sem))
 
 
 def pack_kernel(mt_ref, dz_ref, acode_ref, ascale_ref, out_ref):
@@ -176,7 +179,7 @@
     left = lax.broadcasted_iota(jnp.int32, (DH, 128), 1) < DH
     left8 = left[:8]
 
-    def work(index, lanes, t):
+    def work(index, lanes):
         total = folded(times(mt_ref[0:128, lanes], diagonal(dz_ref[0:DH, lanes], masks)))
         total += folded(times(mt_ref[128:256, lanes], diagonal(dz_ref[DH:128, lanes], masks)))
         scale = column_scale(total)
@@ -192,7 +195,8 @@
             out_ref[head + 1, 0:DH, :] = jnp.where(left, pltpu.roll(a_code[:, cut], DH, 1), code[:, cut]).astype(BF16)
             out_ref[head + 1, DH : DH + 8, :] = jnp.where(left8, pltpu.roll(a_scale[:, cut], DH, 1), scale[:, cut]).astype(BF16)
 
-    run(work, dz_ref.shape[1] // QUAD)
+    for index in range(dz_ref.shape[1] // QUAD):
+        work(index, slice(index * QUAD, (index + 1) * QUAD))
 
 
 def relay_kernel(in_ref, out_ref, map_ref, left_ref, group):
@@ -262,10 +266,11 @@
             out_ref[j + 1, half : half + 8, :] = jnp.where(left[:8], other, scale).astype(BF16)
 
 
-def trail_kernel(rate_ref, *refs):
-    inputs, outputs, (flat_ref, in_sems, out_sems) = refs[:5], refs[5:10], refs[20:]
-    q_ref, k_ref, v_ref, w_ref, dz_ref = refs[10:15]
-    e_ref, wt_ref, kt_ref, t_ref, outer_ref = refs[15:20]
+def trail_kernel(rate_hbm, *refs):
+    inputs, (e_ref, wt_ref), outputs, (rate_ref, rate_sem) = refs[:5], refs[5:7], refs[7:10], refs[10:12]
+    q_ref, k_ref, v_ref, w_ref, dz_ref = refs[12:17]
+    kt_ref, t_ref, outer_ref = refs[17:20]
+    flat_ref, in_sems, out_sems = refs[20:]
     row, col, _ = quad_iota()
     masks = head_masks()
     identity = (row == col).astype(F32).astype(BF16)
@@ -313,15 +318,14 @@
             outer_ref[rows, lanes] = on_dz[128:]
 
     features = k_ref.shape[1]
-    fetch = mover(inputs, refs[10:15], in_sems, features)
-    ship = mover(refs[15:20], outputs, out_sems, features)
-    run(work, features // QUAD, fetch, ship)
-
-
-def direct_kernel(rate_ref, *refs):
-    inputs, outputs, (in_sems, out_sems) = refs[:5], refs[5:7], refs[14:]
-    q_ref, k_ref, dz_ref, e_ref, wt_ref = refs[7:12]
-    gq_ref, part_ref = refs[12:14]
+    fetch = mover(inputs, refs[12:17], in_sems, features)
+    ship = mover(refs[17:20], outputs, out_sems, features)
+    run(work, features // QUAD, fetch, ship, pltpu.make_async_copy(rate_hbm, rate_ref, rate_sem))
+
+
+def direct_kernel(rate_hbm, e_ref, wt_ref, *refs):
+    inputs, outputs, (rate_ref, rate_sem) = refs[:3], refs[3:5], refs[5:7]
+    q_ref, k_ref, dz_ref, gq_ref, part_ref, in_sems, out_sems = refs[7:]
     row, col, _ = quad_iota()
     masks = head_masks()
     upper = (row <= col).astype(F32)
@@ -343,19 +347,15 @@
             part_ref[rows, lanes] = folded(times(both(*split(dpt)), diagonal(q_ref[rows, lanes], masks)))
 
     features = k_ref.shape[1]
-    run(work, features // QUAD, mover(inputs, refs[7:12], in_sems, features), mover(refs[12:14], outputs, out_sems, features))
-
-
-def final_kernel(rate_ref, code_hbm, *refs):
-    inputs, outputs = refs[:7], refs[7:10]
-    k_ref, kt_ref, e_ref, wt_ref, t_ref, outer_ref, part_ref = refs[10:17]
-    gk_ref, gv_ref, start_ref, code_ref, flat_ref, in_sems, out_sems, code_sems = refs[17:]
-
-    def code_copy(i):
-        size = code_ref.shape[0] // CHUNKS
-        part = pl.ds(i * size, size)
-        return pltpu.make_async_copy(code_hbm.at[part], code_ref.at[part], code_sems.at[i])
-
+    fetch = mover(inputs, (q_ref, k_ref, dz_ref), in_sems, features)
+    ship = mover((gq_ref, part_ref), outputs, out_sems, features)
+    run(work, features // QUAD, fetch, ship, pltpu.make_async_copy(rate_hbm, rate_ref, rate_sem))
+
+
+def final_kernel(rate_hbm, code_ref, e_ref, wt_ref, *refs):
+    inputs, outputs, (rate_ref, rate_sem) = refs[:5], refs[5:8], refs[8:10]
+    k_ref, kt_ref, t_ref, outer_ref, part_ref = refs[10:15]
+    gk_ref, gv_ref, start_ref, flat_ref, in_sems, out_sems = refs[15:]
     masks = head_masks()
     half = DH // 2
     low = lax.broadcasted_iota(jnp.int32, (half, 128), 1) < DH
@@ -404,17 +404,9 @@
                 start_ref[pl.ds(head, 8), i * 128 : (i + 1) * 128] = flat_ref[pl.ds(head * half + i, 8, stride=half), :]
 
     features = k_ref.shape[1]
-    start, wait = mover(inputs, refs[10:17], in_sems, features)
-
-    def start_all(i):
-        code_copy(i).start()
-        start(i)
-
-    def wait_all(i):
-        code_copy(i).wait()
-        wait(i)
-
-    run(work, features // QUAD, (start_all, wait_all), mover((gk_ref, gv_ref, start_ref), outputs, out_sems, features))
+    fetch = mover(inputs, refs[10:15], in_sems, features)
+    ship = mover((gk_ref, gv_ref, start_ref), outputs, out_sems, features)
+    run(work, features // QUAD, fetch, ship, pltpu.make_async_copy(rate_hbm, rate_ref, rate_sem))
 
 
 def call(kernel, ins, outs, flops, scratch=(), limit=58):
@@ -422,7 +414,7 @@
     size = sum(a.size * a.dtype.itemsize for a in args) + sum(o.size * o.dtype.itemsize for o, _ in outs)
     return pl.pallas_call(
         kernel,
-        out_shape=tuple(shape for shape, _ in outs),
+        out_shape=tuple(shape if memory is pltpu.VMEM else pltpu.HBM(shape.shape, shape.dtype) for shape, memory in outs),
         in_specs=[pl.BlockSpec(memory_space=memory) for _, memory in ins],
         out_specs=tuple(pl.BlockSpec(memory_space=memory) for _, memory in outs),
         scratch_shapes=list(scratch),
@@ -452,38 +444,39 @@
         return pltpu.SemaphoreType.DMA((count, CHUNKS))
 
     def outside(arrays):
-        return [(a, pltpu.HBM) for a in arrays]
+        return [(a if isinstance(a, jax.ShapeDtypeStruct) else pltpu.with_memory_space_constraint(a, pltpu.HBM), pltpu.HBM) for a in arrays]
 
     def inside(arrays):
         return [(a, pltpu.VMEM) for a in arrays]
 
-    rate = [(inner_rate, pltpu.SMEM)]
     unit = 2 * tokens * features * QUAD
     flat = pltpu.VMEM((heads * DH // 2, 128), F32)
     single, whole, double = array(tokens, F32), array(tokens, BF16), array(2 * tokens, BF16)
+    rate = [pltpu.SMEM(inner_rate.shape, F32), pltpu.SemaphoreType.DMA]
 
     cotangent = lax.ppermute(upstream, "section", [((i + 1) % sections, i) for i in range(sections)])
     dz = cotangent[0]
     acode, ascale, mt = call(
         map_kernel,
-        outside([q, k]) + rate,
+        outside([inner_rate, q, k]),
         inside([array(DH, BF16), array(8, F32), double]),
         8 * unit,
-        buffers([q, k]) + [semaphores(2)],
-        24,
+        rate + buffers([q, k]) + [semaphores(2)],
+        MAP_LIMIT,
     )
     (packed,) = call(
         pack_kernel, inside([mt, dz, acode, ascale]), inside([jax.ShapeDtypeStruct((heads, DH + 8, 128), BF16)]), 2 * unit, (), 24
     )
     arrived = lax.all_to_all(packed, "seq", 0, 0, tiled=True)
     rate_later, _ = lax.optimization_barrier((inner_rate, packed))
-    given, made = [q, k, v, w, dz], [double, double, whole, single, single]
+    given, made = [q, k, v, w, dz], [whole, single, single]
     error, weights, kt, slope, outer = call(
         trail_kernel,
-        [(rate_later, pltpu.SMEM)] + outside(given),
-        outside([apart(a) for a in made]),
+        outside([rate_later] + given),
+        inside([double, double]) + outside([apart(a) for a in made]),
         10 * unit,
-        buffers(given + made) + [flat, semaphores(5), semaphores(5)],
+        rate + buffers(given + made) + [flat, semaphores(5), semaphores(3)],
+        LATE_LIMIT,
     )
     arrived, slope = lax.optimization_barrier((arrived, slope))
     (ends,) = call(
@@ -496,22 +489,22 @@
     )
     returned = lax.all_to_all(ends, "seq", 0, 0, tiled=True)
     rate_later, _ = lax.optimization_barrier((inner_rate, ends))
-    given, held, made = [q, k, dz, error, weights], [whole, whole, whole, double, double], [whole, single]
     grad_q, part = call(
         direct_kernel,
-        [(rate_later, pltpu.SMEM)] + outside(given),
+        outside([rate_later]) + inside([error, weights]) + outside([q, k, dz]),
         outside([whole, apart(single)]),
         10 * unit,
-        buffers(held + made) + [semaphores(5), semaphores(2)],
-    )
-    given, held = [k, kt, error, weights, slope, outer, part], [whole, whole, double, double, single, single, single]
-    made = [whole, whole, array(heads, F32, DH * DH)]
+        rate + buffers([whole, whole, whole, whole, single]) + [semaphores(3), semaphores(2)],
+        LATE_LIMIT,
+    )
+    held, made = [whole, whole, single, single, single], [whole, whole, array(heads, F32, DH * DH)]
     grad_k, grad_v, start = call(
         final_kernel,
-        rate + outside([returned] + given),
+        outside([inner_rate]) + inside([returned, error, weights]) + outside([k, kt, slope, outer, part]),
         outside(made),
         10 * unit,
-        buffers(held + made + [returned]) + [flat, semaphores(7), semaphores(3), pltpu.SemaphoreType.DMA((CHUNKS,))],
+        rate + buffers(held + made) + [flat, semaphores(5), semaphores(3)],
+        LATE_LIMIT,
     )
     return grad_q[None], grad_k[None], grad_v[None], start[None, None]
 

time: 78.6 us -> 74.3 us (0.945)
  Pallas kernels: 42.5 us -> 38.8 us
  local copies, waits for them, and re-layouts: 3.48 us -> 0.01 us
  waiting for transfers between devices: 15.1 us -> 18.2 us
    pallas_call x6, Pallas kernels: 42.5 us -> 38.8 us  [call(): pl.pallas_call(kernel, out_shape=tuple((shape if memory is pltpu.VMEM els...]
    unnamed x10 -> x2, local copies, waits for them, and re-layouts: 3.48 us -> 0.01 us
    all_to_all x1, waiting for transfers between devices: 5.27 us -> 6.9 us  [per_device(): returned = lax.all_to_all(ends, 'seq', 0, 0, tiled=True)]
    all_to_all x1, waiting for transfers between devices: 9.84 us -> 11.3 us  [per_device(): arrived = lax.all_to_all(packed, 'seq', 0, 0, tiled=True)]
  transfers between devices with their start and end apart: 3 -> 3, of which waited for: 2 -> 2; matrix products, arithmetic and copies ran while one was open for 0% -> 0% of each run, Pallas kernels for 32% -> 31%
where the time goes in v2:
time: 74.3 us; the launch traced here: 74 us
  Pallas kernels  38.8 us (52%)
  waiting for transfers between devices  18.2 us (24%)
  starting transfers between devices  16.3 us (22%)
    pallas_call x6, Pallas kernels, call(): pl.pallas_call(kernel, out_shape=tuple((shape if memory is pltpu.VMEM els...  38.8 us
    all_to_all x1, waiting for transfers between devices, per_device(): arrived = lax.all_to_all(packed, 'seq', 0, 0, tiled=True)  11.3 us
    all_to_all x1, starting transfers between devices, per_device(): arrived = lax.all_to_all(packed, 'seq', 0, 0, tiled=True)  11.2 us
    all_to_all x1, waiting for transfers between devices, per_device(): returned = lax.all_to_all(ends, 'seq', 0, 0, tiled=True)  6.9 us
    all_to_all x1, starting transfers between devices, per_device(): returned = lax.all_to_all(ends, 'seq', 0, 0, tiled=True)  5.09 us
  transfers between devices with their start and end apart: 3, of which 2 were waited for; matrix products, arithmetic and copies ran while one was open for 0% of the time, Pallas kernels for 31%

profile of v2, /device:TPU:40, one launch (start us, length us, event | category | flops | bytes accessed | tf_op | source)
XLA Modules:
  0.0 74.0 jit_solution(10007027707975326995)
XLA Ops:
  0.6 0.0 collective-permute-start
  0.7 7.5 %shard_map.93 = (bf16[64,2048]{1,0:T(8,128)(2,1)S(1)}, f32[8,2048]{1,0:T(8,128)S(1)}, bf16[256,2048]{1,0:T(8,128)(2,1)S(1)}) custom-call(f32[1,32]{1,0:T(1,128)} %rate_hbm.5, bf16[128,2048]{1,0:T(8,128)(2,1)} %bitcast.18, bf16[128,2048]{1,0:T(8,128)(2,1)} %bitcast.12), custom_call_target="tpu_custom_call" | custom-call | flops 1073741824 | bytes 2424960 | tf_op jit(solution)/shard_map/pallas_call | solution.py:415
  8.2 0.0 collective-permute-done
  8.2 0.0 copy-start
  8.2 1.5 %shard_map.94 = bf16[32,72,128]{2,1,0:T(8,128)(2,1)} custom-call(bf16[256,2048]{1,0:T(8,128)(2,1)S(1)} %get-tuple-element.21.mt_ref, bf16[128,2048]{1,0:T(8,128)(2,1)S(1)} %bitcast.9, bf16[64,2048]{1,0:T(8,128)(2,1)S(1)} %get-tuple-element.22.acode_ref, f32[8,2048]{1,0:T(8,128)S(1)} %get-tuple-element.23.ascale_ref), custom_call_target="tpu_custom_call" | custom-call | flops 268435456 | bytes 2490368 | tf_op jit(solution)/shard_map/pallas_call | solution.py:415
  9.7 0.0 copy-done
  9.7 11.2 %all-to-all-start = ((bf16[32,72,128]{2,1,0:T(8,128)(2,1)}), bf16[32,72,128]{2,1,0:T(8,128)(2,1)S(1)}, u32[]{:S(2)}, u32[]{:S(2)}) async-start(bf16[32,72,128]{2,1,0:T(8,128)(2,1)} %shard_map.94), calls=%async_computation | async-start | bytes 1179648 | tf_op jit(solution)/shard_map/all_to_all | solution.py:470
  20.9 8.8 %shard_map.95 = (bf16[256,2048]{1,0:T(8,128)(2,1)S(1)}, bf16[256,2048]{1,0:T(8,128)(2,1)S(1)}, bf16[512,512]{1,0:T(8,128)(2,1)}, f32[512,512]{1,0:T(8,128)}, f32[512,512]{1,0:T(8,128)}) custom-call(f32[1,32]{1,0:T(1,128)} %rate_hbm.5, bf16[128,2048]{1,0:T(8,128)(2,1)} %bitcast.19, bf16[128,2048]{1,0:T(8,128)(2,1)} %bitcast.13, bf16[128,2048]{1,0:T(8,128)(2,1)} %bitcast.16, ...), custom_call_target="tpu_custom_call" | custom-call | flops 1342177280 | bytes 7340160 | tf_op jit(solution)/shard_map/pallas_call | solution.py:415
  29.7 11.3 %all-to-all-done.in_ref = bf16[32,72,128]{2,1,0:T(8,128)(2,1)S(1)} async-done(((bf16[32,72,128]{2,1,0:T(8,128)(2,1)}), bf16[32,72,128]{2,1,0:T(8,128)(2,1)S(1)}, u32[]{:S(2)}, u32[]{:S(2)}) %all-to-all-start) | async-done | bytes 589856 | tf_op jit(solution)/shard_map/all_to_all | solution.py:470
  41.1 4.2 %shard_map.96 = bf16[32,40,128]{2,1,0:T(8,128)(2,1)} custom-call(bf16[32,72,128]{2,1,0:T(8,128)(2,1)S(1)} %all-to-all-done.in_ref), custom_call_target="tpu_custom_call" | custom-call | flops 134217728 | bytes 917504 | tf_op jit(solution)/shard_map/pallas_call | solution.py:415
  45.3 5.1 %all-to-all-start.1 = ((bf16[32,40,128]{2,1,0:T(8,128)(2,1)}), bf16[32,40,128]{2,1,0:T(8,128)(2,1)S(1)}, u32[]{:S(2)}, u32[]{:S(2)}) async-start(bf16[32,40,128]{2,1,0:T(8,128)(2,1)} %shard_map.96), calls=%async_computation.1 | async-start | bytes 655360 | tf_op jit(solution)/shard_map/all_to_all | solution.py:490
  50.4 7.0 %shard_map.97 = (bf16[128,2048]{1,0:T(8,128)(2,1)}, f32[512,512]{1,0:T(8,128)}) custom-call(f32[1,32]{1,0:T(1,128)} %rate_hbm.5, bf16[256,2048]{1,0:T(8,128)(2,1)S(1)} %get-tuple-element.28.e_ref, bf16[256,2048]{1,0:T(8,128)(2,1)S(1)} %get-tuple-element.29.wt_ref, bf16[128,2048]{1,0:T(8,128)(2,1)} %bitcast.20, bf16[128,2048]{1,0:T(8,128)(2,1)} %bitcast.14, ...), custom_call_target="tpu_custom_call" | custom-call | flops 1342177280 | bytes 5243008 | tf_op jit(solution)/shard_map/pallas_call | solution.py:415
  57.4 6.9 %all-to-all-done.1.code_ref = bf16[32,40,128]{2,1,0:T(8,128)(2,1)S(1)} async-done(((bf16[32,40,128]{2,1,0:T(8,128)(2,1)}), bf16[32,40,128]{2,1,0:T(8,128)(2,1)S(1)}, u32[]{:S(2)}, u32[]{:S(2)}) %all-to-all-start.1) | async-done | bytes 327712 | tf_op jit(solution)/shard_map/all_to_all | solution.py:490
  64.3 9.7 %shard_map.98 = (bf16[128,2048]{1,0:T(8,128)(2,1)}, bf16[128,2048]{1,0:T(8,128)(2,1)}, f32[32,4096]{1,0:T(8,128)}) custom-call(f32[1,32]{1,0:T(1,128)} %rate_hbm.5, bf16[32,40,128]{2,1,0:T(8,128)(2,1)S(1)} %all-to-all-done.1.code_ref, bf16[256,2048]{1,0:T(8,128)(2,1)S(1)} %get-tuple-element.28.e_ref, bf16[256,2048]{1,0:T(8,128)(2,1)S(1)} %get-tuple-element.29.wt_ref, ...), custom_call_target="tpu_custom_call" | custom-call | flops 1342177280 | bytes 8192128 | tf_op jit(solution)/shard_map/pallas_call | solution.py:415
Async XLA Ops:
  0.6 7.6 %collective-permute-start = (bf16[1,128,2048]{2,1,0:T(8,128)(2,1)}, bf16[1,128,2048]{2,1,0:T(8,128)(2,1)S(1)}, u32[]{:S(2)}, u32[]{:S(2)}) collective-permute-start(bf16[1,128,2048]{2,1,0:T(8,128)(2,1)} %param.9), channel_id=1, source_target_pairs={{32,0},{64,32},{96,64},{128,96},{160,128},{192,160},{224,192},{0,2... | collective-permute-start | bytes 1572872 | tf_op jit(solution)/shard_map/ppermute | solution.py:457
  8.2 1.5 %copy-start = (bf16[1,128,2048]{2,1,0:T(8,128)(2,1)}, bf16[1,128,2048]{2,1,0:T(8,128)(2,1)S(1)}, u32[]{:S(2)}) copy-start(bf16[1,128,2048]{2,1,0:T(8,128)(2,1)S(1)} %collective-permute-done) | copy-start | bytes 1572868
  9.7 31.3 %all-to-all-start = ((bf16[32,72,128]{2,1,0:T(8,128)(2,1)}), bf16[32,72,128]{2,1,0:T(8,128)(2,1)S(1)}, u32[]{:S(2)}, u32[]{:S(2)}) async-start(bf16[32,72,128]{2,1,0:T(8,128)(2,1)} %shard_map.94), calls=%async_computation | async-start | bytes 1179648 | tf_op jit(solution)/shard_map/all_to_all | solution.py:470
  45.3 19.0 %all-to-all-start.1 = ((bf16[32,40,128]{2,1,0:T(8,128)(2,1)}), bf16[32,40,128]{2,1,0:T(8,128)(2,1)S(1)}, u32[]{:S(2)}, u32[]{:S(2)}) async-start(bf16[32,40,128]{2,1,0:T(8,128)(2,1)} %shard_map.96), calls=%async_computation.1 | async-start | bytes 655360 | tf_op jit(solution)/shard_map/all_to_all | solution.py:490

commit v3 on v2

--- a/solution.py
+++ b/solution.py
@@ -206,13 +206,10 @@
     left = lane < DH
     unit = (row == lane).astype(F32)
 
-    def unpack(j, carry):
+    def unpack(j):
         scale = in_ref[j, DH : DH + 8, :].astype(F32)[0:1]
         value = decode(in_ref[j, 0:DH, :].astype(F32), scale)
-        value = jnp.where(left, unit - value, value)
-        map_ref[j] = value
-        left_ref[j] = left_operand(value)
-        return carry
+        return jnp.where(left, unit - value, value)
 
     def left_operand(value):
         hi, lo = split(value)
@@ -226,14 +223,18 @@
         hi, lo = split(value)
         return jnp.concatenate([hi, hi, lo, jnp.zeros_like(lo)], axis=0)
 
-    lax.fori_loop(0, shards, unpack, 0, unroll=4)
     groups = shards // group
-    suffix = [map_ref[g * group + group - 1] for g in range(groups)]
+    suffix = []
+    for g in range(groups):
+        j = g * group + group - 1
+        suffix.append(unpack(j))
+        map_ref[j] = suffix[g]
+        left_ref[j] = left_operand(suffix[g])
     for step in range(group - 2, -1, -1):
         for g in range(groups):
             j = g * group + step
-            own = map_ref[j]
-            suffix[g] = times(left_ref[j], right_operand(suffix[g])) + jnp.where(left, 0.0, own)
+            own = unpack(j)
+            suffix[g] = times(left_operand(own), right_operand(suffix[g])) + jnp.where(left, 0.0, own)
             map_ref[j] = suffix[g]
             left_ref[j] = left_operand(suffix[g])
     ends = [None] * groups
@@ -269,7 +270,7 @@
 def trail_kernel(rate_hbm, *refs):
     inputs, (e_ref, wt_ref), outputs, (rate_ref, rate_sem) = refs[:5], refs[5:7], refs[7:10], refs[10:12]
     q_ref, k_ref, v_ref, w_ref, dz_ref = refs[12:17]
-    kt_ref, t_ref, outer_ref = refs[17:20]
+    gate_ref, t_ref, source_ref = refs[17:20]
     flat_ref, in_sems, out_sems = refs[20:]
     row, col, _ = quad_iota()
     masks = head_masks()
@@ -300,22 +301,28 @@
             hi_rows, lo_rows = slice(b * 128, b * 128 + 64), slice(b * 128 + 64, b * 128 + 128)
             k = k_ref[rows, lanes]
             w_hi, w_lo = split(weight)
-            wt_ref[hi_rows, lanes] = w_hi
-            wt_ref[lo_rows, lanes] = w_lo
-            error = times(k, diagonal(w_hi, masks)) + times(k, diagonal(w_lo, masks)) - v_ref[rows, lanes].astype(F32)
+            w_block, w_low_block = diagonal(w_hi, masks), diagonal(w_lo, masks)
+            wt_ref[hi_rows, lanes] = times_t(identity, w_block).astype(BF16)
+            wt_ref[lo_rows, lanes] = times_t(identity, w_low_block).astype(BF16)
+            error = times(k, w_block) + times(k, w_low_block) - v_ref[rows, lanes].astype(F32)
             e_hi, e_lo = split(error)
             e_ref[hi_rows, lanes] = e_hi
             e_ref[lo_rows, lanes] = e_lo
-            kt = times_t(identity, diagonal(k, masks)).astype(BF16)
-            kt_ref[rows, lanes] = kt
+            k_block = diagonal(k, masks)
+            kt = times_t(identity, k_block).astype(BF16)
+            gate_hi, gate_lo = split(rate * times(kt, k_block))
+            gate_ref[hi_rows, lanes] = gate_hi
+            gate_ref[lo_rows, lanes] = gate_lo
             if b == 0:
                 weight = weight - rate * (times(kt, diagonal(e_hi, masks)) + times(kt, diagonal(e_lo, masks)))
             on_q = times_t(both(k, identity), diagonal(q_ref[rows, lanes], masks))
             st_hi, st_lo = split(on_q[:DH] * upper)
             qt = on_q[DH:].astype(BF16)
             on_dz = times(jnp.concatenate([st_hi, st_lo, qt], axis=0), diagonal(dz_ref[rows, lanes], masks))
-            t_ref[rows, lanes] = on_dz[:DH] + on_dz[DH:128]
-            outer_ref[rows, lanes] = on_dz[128:]
+            slope = on_dz[:DH] + on_dz[DH:128]
+            t_ref[rows, lanes] = slope
+            t_hi, t_lo = split(slope)
+            source_ref[rows, lanes] = on_dz[128:] - rate * (times(kt, diagonal(t_hi, masks)) + times(kt, diagonal(t_lo, masks)))
 
     features = k_ref.shape[1]
     fetch = mover(inputs, refs[12:17], in_sems, features)
@@ -341,7 +348,7 @@
             dpt = folded(times_t(e_ref[two, lanes], diagonal(dz, masks))) * (-rate * upper)
             dp = times_t(dz, diagonal(e_ref[hi_rows, lanes], masks)) + times_t(dz, diagonal(e_ref[lo_rows, lanes], masks))
             dp = dp * (-rate * lower)
-            grad = times_t(dz, diagonal(wt_ref[hi_rows, lanes], masks)) + times_t(dz, diagonal(wt_ref[lo_rows, lanes], masks))
+            grad = times(dz, diagonal(wt_ref[hi_rows, lanes], masks)) + times(dz, diagonal(wt_ref[lo_rows, lanes], masks))
             grad += folded(times(both(*split(dp)), diagonal(k_ref[rows, lanes], masks)))
             gq_ref[rows, lanes] = grad.astype(BF16)
             part_ref[rows, lanes] = folded(times(both(*split(dpt)), diagonal(q_ref[rows, lanes], masks)))
@@ -354,7 +361,7 @@
 
 def final_kernel(rate_hbm, code_ref, e_ref, wt_ref, *refs):
     inputs, outputs, (rate_ref, rate_sem) = refs[:5], refs[5:8], refs[8:10]
-    k_ref, kt_ref, t_ref, outer_ref, part_ref = refs[10:15]
+    k_ref, gate_ref, t_ref, source_ref, part_ref = refs[10:15]
     gk_ref, gv_ref, start_ref, flat_ref, in_sems, out_sems = refs[15:]
     masks = head_masks()
     half = DH // 2
@@ -379,18 +386,19 @@
             hi_rows, lo_rows = slice(b * 128, b * 128 + 64), slice(b * 128 + 64, b * 128 + 128)
             g_hi, g_lo = split(adjoint)
             g_block, g_low_block = diagonal(g_hi, masks), diagonal(g_lo, masks)
-            k = k_ref[rows, lanes]
-            slope = t_ref[rows, lanes] + times(k, g_block) + times(k, g_low_block)
+            k, gate = k_ref[rows, lanes], gate_ref[two, lanes]
+            high = times(jnp.concatenate([k, gate], axis=0), g_block)
+            low_part = times(jnp.concatenate([k, gate[:DH]], axis=0), g_low_block)
+            slope = t_ref[rows, lanes] + high[:DH] + low_part[:DH]
+            adjoint = adjoint - (folded(high[DH:]) + low_part[DH:]) + source_ref[rows, lanes]
             grad_error = -rate * slope
             gv_ref[rows, lanes] = (-grad_error).astype(BF16)
             d_hi, d_lo = split(grad_error)
-            kt = kt_ref[rows, lanes]
             grad = part_ref[rows, lanes]
-            grad += folded(times_t(both(d_hi, d_lo), diagonal(wt_ref[hi_rows, lanes], masks)))
-            grad += times_t(d_hi, diagonal(wt_ref[lo_rows, lanes], masks))
+            grad += folded(times(both(d_hi, d_lo), diagonal(wt_ref[hi_rows, lanes], masks)))
+            grad += times(d_hi, diagonal(wt_ref[lo_rows, lanes], masks))
             on_g = folded(times_t(e_ref[two, lanes], g_block)) + times_t(e_ref[hi_rows, lanes], g_low_block)
             gk_ref[rows, lanes] = (grad - rate * on_g).astype(BF16)
-            adjoint = adjoint + outer_ref[rows, lanes] + times(kt, diagonal(d_hi, masks)) + times(kt, diagonal(d_lo, masks))
         for p in range(PAIRS):
             first = pl.multiple_of((index * PAIRS + p) * DH, DH)
             flat_ref[pl.ds(first, DH), :] = adjoint[:, p * 128 : p * 128 + 128]
@@ -469,8 +477,8 @@
     )
     arrived = lax.all_to_all(packed, "seq", 0, 0, tiled=True)
     rate_later, _ = lax.optimization_barrier((inner_rate, packed))
-    given, made = [q, k, v, w, dz], [whole, single, single]
-    error, weights, kt, slope, outer = call(
+    given, made = [q, k, v, w, dz], [double, single, single]
+    error, weights, gate, slope, source = call(
         trail_kernel,
         outside([rate_later] + given),
         inside([double, double]) + outside([apart(a) for a in made]),
@@ -497,10 +505,10 @@
         rate + buffers([whole, whole, whole, whole, single]) + [semaphores(3), semaphores(2)],
         LATE_LIMIT,
     )
-    held, made = [whole, whole, single, single, single], [whole, whole, array(heads, F32, DH * DH)]
+    held, made = [whole, double, single, single, single], [whole, whole, array(heads, F32, DH * DH)]
     grad_k, grad_v, start = call(
         final_kernel,
-        outside([inner_rate]) + inside([returned, error, weights]) + outside([k, kt, slope, outer, part]),
+        outside([inner_rate]) + inside([returned, error, weights]) + outside([k, gate, slope, source, part]),
         outside(made),
         10 * unit,
         rate + buffers(held + made) + [flat, semaphores(5), semaphores(3)],

time: 74.3 us -> 71 us (0.956)
  waiting for transfers between devices: 18.2 us -> 13.9 us
  Pallas kernels: 38.8 us -> 39.8 us
    all_to_all x1, waiting for transfers between devices: 11.3 us -> 6.51 us  [per_device(): arrived = lax.all_to_all(packed, 'seq', 0, 0, tiled=True)]
    pallas_call x6, Pallas kernels: 38.8 us -> 39.8 us  [call(): pl.pallas_call(kernel, out_shape=tuple((shape if memory is pltpu.VMEM els...]
  transfers between devices with their start and end apart: 3 -> 3, of which waited for: 2 -> 2; matrix products, arithmetic and copies ran while one was open for 0% -> 0% of each run, Pallas kernels for 31% -> 39%
where the time goes in v3:
time: 71 us; the launch traced here: 70.6 us
  Pallas kernels  39.8 us (56%)
  starting transfers between devices  16.3 us (23%)
  waiting for transfers between devices  13.9 us (20%)
    pallas_call x6, Pallas kernels, call(): pl.pallas_call(kernel, out_shape=tuple((shape if memory is pltpu.VMEM els...  39.8 us
    all_to_all x1, starting transfers between devices, per_device(): arrived = lax.all_to_all(packed, 'seq', 0, 0, tiled=True)  11.2 us
    all_to_all x1, waiting for transfers between devices, per_device(): returned = lax.all_to_all(ends, 'seq', 0, 0, tiled=True)  7.34 us
    all_to_all x1, waiting for transfers between devices, per_device(): arrived = lax.all_to_all(packed, 'seq', 0, 0, tiled=True)  6.51 us
    all_to_all x1, starting transfers between devices, per_device(): returned = lax.all_to_all(ends, 'seq', 0, 0, tiled=True)  5.09 us
  transfers between devices with their start and end apart: 3, of which 2 were waited for; matrix products, arithmetic and copies ran while one was open for 0% of the time, Pallas kernels for 39%

profile of v3, /device:TPU:40, one launch (start us, length us, event | category | flops | bytes accessed | tf_op | source)
XLA Modules:
  0.0 70.6 jit_solution(16963460330241135808)
XLA Ops:
  0.6 0.0 collective-permute-start
  0.7 7.5 %shard_map.93 = (bf16[64,2048]{1,0:T(8,128)(2,1)S(1)}, f32[8,2048]{1,0:T(8,128)S(1)}, bf16[256,2048]{1,0:T(8,128)(2,1)S(1)}) custom-call(f32[1,32]{1,0:T(1,128)} %rate_hbm.5, bf16[128,2048]{1,0:T(8,128)(2,1)} %bitcast.18, bf16[128,2048]{1,0:T(8,128)(2,1)} %bitcast.12), custom_call_target="tpu_custom_call" | custom-call | flops 1073741824 | bytes 2424960 | tf_op jit(solution)/shard_map/pallas_call | solution.py:423
  8.2 0.0 collective-permute-done
  8.2 0.0 copy-start
  8.2 1.5 %shard_map.94 = bf16[32,72,128]{2,1,0:T(8,128)(2,1)} custom-call(bf16[256,2048]{1,0:T(8,128)(2,1)S(1)} %get-tuple-element.21.mt_ref, bf16[128,2048]{1,0:T(8,128)(2,1)S(1)} %bitcast.9, bf16[64,2048]{1,0:T(8,128)(2,1)S(1)} %get-tuple-element.22.acode_ref, f32[8,2048]{1,0:T(8,128)S(1)} %get-tuple-element.23.ascale_ref), custom_call_target="tpu_custom_call" | custom-call | flops 268435456 | bytes 2490368 | tf_op jit(solution)/shard_map/pallas_call | solution.py:423
  9.8 0.0 copy-done
  9.8 11.2 %all-to-all-start = ((bf16[32,72,128]{2,1,0:T(8,128)(2,1)}), bf16[32,72,128]{2,1,0:T(8,128)(2,1)S(1)}, u32[]{:S(2)}, u32[]{:S(2)}) async-start(bf16[32,72,128]{2,1,0:T(8,128)(2,1)} %shard_map.94), calls=%async_computation | async-start | bytes 1179648 | tf_op jit(solution)/shard_map/all_to_all | solution.py:478
  20.9 13.6 %shard_map.95 = (bf16[256,2048]{1,0:T(8,128)(2,1)S(1)}, bf16[256,2048]{1,0:T(8,128)(2,1)S(1)}, bf16[1024,512]{1,0:T(8,128)(2,1)}, f32[512,512]{1,0:T(8,128)}, f32[512,512]{1,0:T(8,128)}) custom-call(f32[1,32]{1,0:T(1,128)} %rate_hbm.5, bf16[128,2048]{1,0:T(8,128)(2,1)} %bitcast.19, bf16[128,2048]{1,0:T(8,128)(2,1)} %bitcast.13, bf16[128,2048]{1,0:T(8,128)(2,1)} %bitcast.16, ...), custom_call_target="tpu_custom_call" | custom-call | flops 1342177280 | bytes 7864448 | tf_op jit(solution)/shard_map/pallas_call | solution.py:423
  34.6 6.5 %all-to-all-done.in_ref = bf16[32,72,128]{2,1,0:T(8,128)(2,1)S(1)} async-done(((bf16[32,72,128]{2,1,0:T(8,128)(2,1)}), bf16[32,72,128]{2,1,0:T(8,128)(2,1)S(1)}, u32[]{:S(2)}, u32[]{:S(2)}) %all-to-all-start) | async-done | bytes 589856 | tf_op jit(solution)/shard_map/all_to_all | solution.py:478
  41.1 3.2 %shard_map.96 = bf16[32,40,128]{2,1,0:T(8,128)(2,1)} custom-call(bf16[32,72,128]{2,1,0:T(8,128)(2,1)S(1)} %all-to-all-done.in_ref), custom_call_target="tpu_custom_call" | custom-call | flops 134217728 | bytes 917504 | tf_op jit(solution)/shard_map/pallas_call | solution.py:423
  44.3 5.1 %all-to-all-start.1 = ((bf16[32,40,128]{2,1,0:T(8,128)(2,1)}), bf16[32,40,128]{2,1,0:T(8,128)(2,1)S(1)}, u32[]{:S(2)}, u32[]{:S(2)}) async-start(bf16[32,40,128]{2,1,0:T(8,128)(2,1)} %shard_map.96), calls=%async_computation.1 | async-start | bytes 655360 | tf_op jit(solution)/shard_map/all_to_all | solution.py:498
  49.4 6.5 %shard_map.97 = (bf16[128,2048]{1,0:T(8,128)(2,1)}, f32[512,512]{1,0:T(8,128)}) custom-call(f32[1,32]{1,0:T(1,128)} %rate_hbm.5, bf16[256,2048]{1,0:T(8,128)(2,1)S(1)} %get-tuple-element.28.e_ref, bf16[256,2048]{1,0:T(8,128)(2,1)S(1)} %get-tuple-element.29.wt_ref, bf16[128,2048]{1,0:T(8,128)(2,1)} %bitcast.20, bf16[128,2048]{1,0:T(8,128)(2,1)} %bitcast.14, ...), custom_call_target="tpu_custom_call" | custom-call | flops 1342177280 | bytes 5243008 | tf_op jit(solution)/shard_map/pallas_call | solution.py:423
  55.9 7.3 %all-to-all-done.1.code_ref = bf16[32,40,128]{2,1,0:T(8,128)(2,1)S(1)} async-done(((bf16[32,40,128]{2,1,0:T(8,128)(2,1)}), bf16[32,40,128]{2,1,0:T(8,128)(2,1)S(1)}, u32[]{:S(2)}, u32[]{:S(2)}) %all-to-all-start.1) | async-done | bytes 327712 | tf_op jit(solution)/shard_map/all_to_all | solution.py:498
  63.3 7.3 %shard_map.98 = (bf16[128,2048]{1,0:T(8,128)(2,1)}, bf16[128,2048]{1,0:T(8,128)(2,1)}, f32[32,4096]{1,0:T(8,128)}) custom-call(f32[1,32]{1,0:T(1,128)} %rate_hbm.5, bf16[32,40,128]{2,1,0:T(8,128)(2,1)S(1)} %all-to-all-done.1.code_ref, bf16[256,2048]{1,0:T(8,128)(2,1)S(1)} %get-tuple-element.28.e_ref, bf16[256,2048]{1,0:T(8,128)(2,1)S(1)} %get-tuple-element.29.wt_ref, ...), custom_call_target="tpu_custom_call" | custom-call | flops 1342177280 | bytes 8716416 | tf_op jit(solution)/shard_map/pallas_call | solution.py:423
Async XLA Ops:
  0.6 7.6 %collective-permute-start = (bf16[1,128,2048]{2,1,0:T(8,128)(2,1)}, bf16[1,128,2048]{2,1,0:T(8,128)(2,1)S(1)}, u32[]{:S(2)}, u32[]{:S(2)}) collective-permute-start(bf16[1,128,2048]{2,1,0:T(8,128)(2,1)} %param.9), channel_id=1, source_target_pairs={{32,0},{64,32},{96,64},{128,96},{160,128},{192,160},{224,192},{0,2... | collective-permute-start | bytes 1572872 | tf_op jit(solution)/shard_map/ppermute | solution.py:465
  8.2 1.6 %copy-start = (bf16[1,128,2048]{2,1,0:T(8,128)(2,1)}, bf16[1,128,2048]{2,1,0:T(8,128)(2,1)S(1)}, u32[]{:S(2)}) copy-start(bf16[1,128,2048]{2,1,0:T(8,128)(2,1)S(1)} %collective-permute-done) | copy-start | bytes 1572868
  9.8 31.3 %all-to-all-start = ((bf16[32,72,128]{2,1,0:T(8,128)(2,1)}), bf16[32,72,128]{2,1,0:T(8,128)(2,1)S(1)}, u32[]{:S(2)}, u32[]{:S(2)}) async-start(bf16[32,72,128]{2,1,0:T(8,128)(2,1)} %shard_map.94), calls=%async_computation | async-start | bytes 1179648 | tf_op jit(solution)/shard_map/all_to_all | solution.py:478
  44.3 19.0 %all-to-all-start.1 = ((bf16[32,40,128]{2,1,0:T(8,128)(2,1)}), bf16[32,40,128]{2,1,0:T(8,128)(2,1)S(1)}, u32[]{:S(2)}, u32[]{:S(2)}) async-start(bf16[32,40,128]{2,1,0:T(8,128)(2,1)} %shard_map.96), calls=%async_computation.1 | async-start | bytes 655360 | tf_op jit(solution)/shard_map/all_to_all | solution.py:498

commit v4 on v3

--- a/solution.py
+++ b/solution.py
@@ -13,6 +13,7 @@
 HEADS = QUAD // DH
 F32 = jnp.float32
 BF16 = jnp.bfloat16
+JOINT = 2
 CHUNKS = 4
 MAP_LIMIT = 24
 LATE_LIMIT = 24
@@ -106,28 +107,30 @@
     return start, wait
 
 
-def run(work, count, fetch, ship=None, first=None):
+def run(work, count, fetch, ship=None, first=None, joint=JOINT):
     each = count // CHUNKS
     first.start()
-    fetch[0](0)
-    fetch[0](1)
+    for i in range(min(2 * joint, CHUNKS)):
+        fetch[0](i)
     first.wait()
 
-    def body(i, carry):
-        fetch[1](i)
-
-        @pl.when(i + 2 < CHUNKS)
-        def _():
-            fetch[0](i + 2)
-
-        for t in range(each):
-            index = i * each + t
-            work(index, pl.ds(pl.multiple_of(index * QUAD, QUAD), QUAD), t)
-        if ship is not None:
-            ship[0](i)
+    def body(n, carry):
+        for m in range(joint):
+            i = n * joint + m
+            fetch[1](i)
+
+            @pl.when(i + 2 * joint < CHUNKS)
+            def _():
+                fetch[0](i + 2 * joint)
+
+        for t in range(each * joint):
+            index = n * each * joint + t
+            work(index, pl.ds(pl.multiple_of(index * QUAD, QUAD), QUAD), t % each)
+            if ship is not None and t % each == each - 1:
+                ship[0](n * joint + t // each)
         return carry
 
-    lax.fori_loop(0, CHUNKS, body, 0)
+    lax.fori_loop(0, CHUNKS // joint, body, 0)
     if ship is not None:
         for i in range(CHUNKS):
             ship[1](i)
@@ -223,6 +226,12 @@
         hi, lo = split(value)
         return jnp.concatenate([hi, hi, lo, jnp.zeros_like(lo)], axis=0)
 
+    def compose(own, behind):
+        return times(left_operand(own), right_operand(behind)) + jnp.where(left, 0.0, own)
+
+    def apply(own, end):
+        return times(left_operand(own), right_operand(end)) + own
+
     groups = shards // group
     suffix = []
     for g in range(groups):
@@ -233,15 +242,22 @@
     for step in range(group - 2, -1, -1):
         for g in range(groups):
             j = g * group + step
-            own = unpack(j)
-            suffix[g] = times(left_operand(own), right_operand(suffix[g])) + jnp.where(left, 0.0, own)
+            suffix[g] = compose(unpack(j), suffix[g])
             map_ref[j] = suffix[g]
             left_ref[j] = left_operand(suffix[g])
+    runs = groups // group
+    for step in range(group - 2, -1, -1):
+        for u in range(runs):
+            g = u * group + step
+            suffix[g] = compose(suffix[g], suffix[g + 1])
     ends = [None] * groups
-    ends[groups - 1] = jnp.zeros((DH, 128), F32)
-    for g in range(groups - 2, -1, -1):
-        j = (g + 1) * group
-        ends[g] = times(left_ref[j], right_operand(ends[g + 1])) + map_ref[j]
+    end = None
+    for u in range(runs - 1, -1, -1):
+        first, last = u * group, u * group + group - 1
+        for g in range(first, last):
+            ends[g] = suffix[g + 1] if end is None else apply(suffix[g + 1], end)
+        ends[last] = jnp.zeros((DH, 128), F32) if end is None else end
+        end = suffix[first] if end is None else apply(suffix[first], end)
     for g in range(groups):
         right = right_operand(ends[g])
         found = []
@@ -268,10 +284,10 @@
 
 
 def trail_kernel(rate_hbm, *refs):
-    inputs, (e_ref, wt_ref), outputs, (rate_ref, rate_sem) = refs[:5], refs[5:7], refs[7:10], refs[10:12]
+    inputs, e_ref, outputs, (rate_ref, rate_sem) = refs[:5], refs[5], refs[6:10], refs[10:12]
     q_ref, k_ref, v_ref, w_ref, dz_ref = refs[12:17]
-    gate_ref, t_ref, source_ref = refs[17:20]
-    flat_ref, in_sems, out_sems = refs[20:]
+    weight_ref, gate_ref, t_ref, source_ref = refs[17:21]
+    flat_ref, in_sems, out_sems = refs[21:]
     row, col, _ = quad_iota()
     masks = head_masks()
     identity = (row == col).astype(F32).astype(BF16)
@@ -302,8 +318,8 @@
             k = k_ref[rows, lanes]
             w_hi, w_lo = split(weight)
             w_block, w_low_block = diagonal(w_hi, masks), diagonal(w_lo, masks)
-            wt_ref[hi_rows, lanes] = times_t(identity, w_block).astype(BF16)
-            wt_ref[lo_rows, lanes] = times_t(identity, w_low_block).astype(BF16)
+            weight_ref[hi_rows, lanes] = w_hi
+            weight_ref[lo_rows, lanes] = w_lo
             error = times(k, w_block) + times(k, w_low_block) - v_ref[rows, lanes].astype(F32)
             e_hi, e_lo = split(error)
             e_ref[hi_rows, lanes] = e_hi
@@ -326,15 +342,16 @@
 
     features = k_ref.shape[1]
     fetch = mover(inputs, refs[12:17], in_sems, features)
-    ship = mover(refs[17:20], outputs, out_sems, features)
+    ship = mover(refs[17:21], outputs, out_sems, features)
     run(work, features // QUAD, fetch, ship, pltpu.make_async_copy(rate_hbm, rate_ref, rate_sem))
 
 
-def direct_kernel(rate_hbm, e_ref, wt_ref, *refs):
-    inputs, outputs, (rate_ref, rate_sem) = refs[:3], refs[3:5], refs[5:7]
-    q_ref, k_ref, dz_ref, gq_ref, part_ref, in_sems, out_sems = refs[7:]
+def direct_kernel(rate_hbm, e_ref, *refs):
+    inputs, outputs, wt_ref, (rate_ref, rate_sem) = refs[:4], refs[4:6], refs[6], refs[7:9]
+    q_ref, k_ref, dz_ref, weight_ref, gq_ref, part_ref, in_sems, out_sems = refs[9:]
     row, col, _ = quad_iota()
     masks = head_masks()
+    identity = (row == col).astype(F32).astype(BF16)
     upper = (row <= col).astype(F32)
     lower = (row >= col).astype(F32)
 
@@ -348,13 +365,18 @@
             dpt = folded(times_t(e_ref[two, lanes], diagonal(dz, masks))) * (-rate * upper)
             dp = times_t(dz, diagonal(e_ref[hi_rows, lanes], masks)) + times_t(dz, diagonal(e_ref[lo_rows, lanes], masks))
             dp = dp * (-rate * lower)
-            grad = times(dz, diagonal(wt_ref[hi_rows, lanes], masks)) + times(dz, diagonal(wt_ref[lo_rows, lanes], masks))
+            left = both(dz, identity)
+            high = times_t(left, diagonal(weight_ref[hi_rows, lanes], masks))
+            low = times_t(left, diagonal(weight_ref[lo_rows, lanes], masks))
+            wt_ref[hi_rows, lanes] = high[DH:].astype(BF16)
+            wt_ref[lo_rows, lanes] = low[DH:].astype(BF16)
+            grad = high[:DH] + low[:DH]
             grad += folded(times(both(*split(dp)), diagonal(k_ref[rows, lanes], masks)))
             gq_ref[rows, lanes] = grad.astype(BF16)
             part_ref[rows, lanes] = folded(times(both(*split(dpt)), diagonal(q_ref[rows, lanes], masks)))
 
     features = k_ref.shape[1]
-    fetch = mover(inputs, (q_ref, k_ref, dz_ref), in_sems, features)
+    fetch = mover(inputs, (q_ref, k_ref, dz_ref, weight_ref), in_sems, features)
     ship = mover((gq_ref, part_ref), outputs, out_sems, features)
     run(work, features // QUAD, fetch, ship, pltpu.make_async_copy(rate_hbm, rate_ref, rate_sem))
 
@@ -477,18 +499,18 @@
     )
     arrived = lax.all_to_all(packed, "seq", 0, 0, tiled=True)
     rate_later, _ = lax.optimization_barrier((inner_rate, packed))
-    given, made = [q, k, v, w, dz], [double, single, single]
+    given, made = [q, k, v, w, dz], [double, double, single, single]
     error, weights, gate, slope, source = call(
         trail_kernel,
         outside([rate_later] + given),
-        inside([double, double]) + outside([apart(a) for a in made]),
+        inside([double]) + outside([apart(a) for a in made]),
         10 * unit,
-        rate + buffers(given + made) + [flat, semaphores(5), semaphores(3)],
+        rate + buffers(given + made) + [flat, semaphores(5), semaphores(4)],
         LATE_LIMIT,
     )
     arrived, slope = lax.optimization_barrier((arrived, slope))
     (ends,) = call(
-        partial(relay_kernel, group=8),
+        partial(relay_kernel, group=4),
         inside([arrived]),
         inside([jax.ShapeDtypeStruct((shards, DH // 2 + 8, 128), BF16)]),
         unit,
@@ -497,18 +519,18 @@
     )
     returned = lax.all_to_all(ends, "seq", 0, 0, tiled=True)
     rate_later, _ = lax.optimization_barrier((inner_rate, ends))
-    grad_q, part = call(
+    grad_q, part, turned = call(
         direct_kernel,
-        outside([rate_later]) + inside([error, weights]) + outside([q, k, dz]),
-        outside([whole, apart(single)]),
+        outside([rate_later]) + inside([error]) + outside([q, k, dz, weights]),
+        outside([whole, apart(single)]) + inside([double]),
         10 * unit,
-        rate + buffers([whole, whole, whole, whole, single]) + [semaphores(3), semaphores(2)],
+        rate + buffers([whole, whole, whole, double, whole, single]) + [semaphores(4), semaphores(2)],
         LATE_LIMIT,
     )
     held, made = [whole, double, single, single, single], [whole, whole, array(heads, F32, DH * DH)]
     grad_k, grad_v, start = call(
         final_kernel,
-        outside([inner_rate]) + inside([returned, error, weights]) + outside([k, gate, slope, source, part]),
+        outside([inner_rate]) + inside([returned, error, turned]) + outside([k, gate, slope, source, part]),
         outside(made),
         10 * unit,
         rate + buffers(held + made) + [flat, semaphores(5), semaphores(3)],

time: 71 us -> 70.5 us (level)
  Pallas kernels: 39.8 us -> 38.2 us
  waiting for transfers between devices: 13.9 us -> 14.8 us
    pallas_call x6, Pallas kernels: 39.8 us -> 38.2 us  [call(): pl.pallas_call(kernel, out_shape=tuple((shape if memory is pltpu.VMEM els...]
    all_to_all x1, waiting for transfers between devices: 6.51 us -> 8.05 us  [per_device(): arrived = lax.all_to_all(packed, 'seq', 0, 0, tiled=True)]
  transfers between devices with their start and end apart: 3 -> 3, of which waited for: 2 -> 2; matrix products, arithmetic and copies ran while one was open for 0% -> 0% of each run, Pallas kernels for 39% -> 38%
where the time goes in v4:
time: 70.5 us; the launch traced here: 70.1 us
  Pallas kernels  38.2 us (54%)
  starting transfers between devices  16.4 us (23%)
  waiting for transfers between devices  14.8 us (21%)
    pallas_call x6, Pallas kernels, call(): pl.pallas_call(kernel, out_shape=tuple((shape if memory is pltpu.VMEM els...  38.2 us
    all_to_all x1, starting transfers between devices, per_device(): arrived = lax.all_to_all(packed, 'seq', 0, 0, tiled=True)  11.2 us
    all_to_all x1, waiting for transfers between devices, per_device(): arrived = lax.all_to_all(packed, 'seq', 0, 0, tiled=True)  8.05 us
    all_to_all x1, waiting for transfers between devices, per_device(): returned = lax.all_to_all(ends, 'seq', 0, 0, tiled=True)  6.74 us
    all_to_all x1, starting transfers between devices, per_device(): returned = lax.all_to_all(ends, 'seq', 0, 0, tiled=True)  5.23 us
  transfers between devices with their start and end apart: 3, of which 2 were waited for; matrix products, arithmetic and copies ran while one was open for 0% of the time, Pallas kernels for 38%

profile of v4, /device:TPU:40, one launch (start us, length us, event | category | flops | bytes accessed | tf_op | source)
XLA Modules:
  0.0 70.1 jit_solution(9244962634327701151)
XLA Ops:
  0.6 0.0 collective-permute-start
  0.7 7.3 %shard_map.93 = (bf16[64,2048]{1,0:T(8,128)(2,1)S(1)}, f32[8,2048]{1,0:T(8,128)S(1)}, bf16[256,2048]{1,0:T(8,128)(2,1)S(1)}) custom-call(f32[1,32]{1,0:T(1,128)} %rate_hbm.5, bf16[128,2048]{1,0:T(8,128)(2,1)} %bitcast.18, bf16[128,2048]{1,0:T(8,128)(2,1)} %bitcast.12), custom_call_target="tpu_custom_call" | custom-call | flops 1073741824 | bytes 2424960 | tf_op jit(solution)/shard_map/pallas_call | solution.py:445
  8.0 0.0 collective-permute-done
  8.0 0.0 copy-start
  8.0 1.5 %shard_map.94 = bf16[32,72,128]{2,1,0:T(8,128)(2,1)} custom-call(bf16[256,2048]{1,0:T(8,128)(2,1)S(1)} %get-tuple-element.22.mt_ref, bf16[128,2048]{1,0:T(8,128)(2,1)S(1)} %bitcast.9, bf16[64,2048]{1,0:T(8,128)(2,1)S(1)} %get-tuple-element.23.acode_ref, f32[8,2048]{1,0:T(8,128)S(1)} %get-tuple-element.24.ascale_ref), custom_call_target="tpu_custom_call" | custom-call | flops 268435456 | bytes 2490368 | tf_op jit(solution)/shard_map/pallas_call | solution.py:445
  9.5 0.0 copy-done
  9.6 11.2 %all-to-all-start = ((bf16[32,72,128]{2,1,0:T(8,128)(2,1)}), bf16[32,72,128]{2,1,0:T(8,128)(2,1)S(1)}, u32[]{:S(2)}, u32[]{:S(2)}) async-start(bf16[32,72,128]{2,1,0:T(8,128)(2,1)} %shard_map.94), calls=%async_computation | async-start | bytes 1179648 | tf_op jit(solution)/shard_map/all_to_all | solution.py:500
  20.8 12.0 %shard_map.95 = (bf16[256,2048]{1,0:T(8,128)(2,1)S(1)}, bf16[1024,512]{1,0:T(8,128)(2,1)}, bf16[1024,512]{1,0:T(8,128)(2,1)}, f32[512,512]{1,0:T(8,128)}, f32[512,512]{1,0:T(8,128)}) custom-call(f32[1,32]{1,0:T(1,128)} %rate_hbm.5, bf16[128,2048]{1,0:T(8,128)(2,1)} %bitcast.19, bf16[128,2048]{1,0:T(8,128)(2,1)} %bitcast.13, bf16[128,2048]{1,0:T(8,128)(2,1)} %bitcast.16, ...), custom_call_target="tpu_custom_call" | custom-call | flops 1342177280 | bytes 7864448 | tf_op jit(solution)/shard_map/pallas_call | solution.py:445
  32.7 8.0 %all-to-all-done.in_ref = bf16[32,72,128]{2,1,0:T(8,128)(2,1)S(1)} async-done(((bf16[32,72,128]{2,1,0:T(8,128)(2,1)}), bf16[32,72,128]{2,1,0:T(8,128)(2,1)S(1)}, u32[]{:S(2)}, u32[]{:S(2)}) %all-to-all-start) | async-done | bytes 589856 | tf_op jit(solution)/shard_map/all_to_all | solution.py:500
  40.8 3.0 %shard_map.96 = bf16[32,40,128]{2,1,0:T(8,128)(2,1)} custom-call(bf16[32,72,128]{2,1,0:T(8,128)(2,1)S(1)} %all-to-all-done.in_ref), custom_call_target="tpu_custom_call" | custom-call | flops 134217728 | bytes 917504 | tf_op jit(solution)/shard_map/pallas_call | solution.py:445
  43.7 5.2 %all-to-all-start.1 = ((bf16[32,40,128]{2,1,0:T(8,128)(2,1)}), bf16[32,40,128]{2,1,0:T(8,128)(2,1)S(1)}, u32[]{:S(2)}, u32[]{:S(2)}) async-start(bf16[32,40,128]{2,1,0:T(8,128)(2,1)} %shard_map.96), calls=%async_computation.1 | async-start | bytes 655360 | tf_op jit(solution)/shard_map/all_to_all | solution.py:520
  49.0 7.1 %shard_map.97 = (bf16[128,2048]{1,0:T(8,128)(2,1)}, f32[512,512]{1,0:T(8,128)}, bf16[256,2048]{1,0:T(8,128)(2,1)S(1)}) custom-call(f32[1,32]{1,0:T(1,128)} %rate_hbm.5, bf16[256,2048]{1,0:T(8,128)(2,1)S(1)} %get-tuple-element.29.e_ref, bf16[128,2048]{1,0:T(8,128)(2,1)} %bitcast.20, bf16[128,2048]{1,0:T(8,128)(2,1)} %bitcast.14, bf16[128,2048]{1,0:T(8,128)(2,1)} %bitcast.11, ...), custom_call_target="tpu_custom_call" | custom-call | flops 1342177280 | bytes 6291584 | tf_op jit(solution)/shard_map/pallas_call | solution.py:445
  56.1 6.7 %all-to-all-done.1.code_ref = bf16[32,40,128]{2,1,0:T(8,128)(2,1)S(1)} async-done(((bf16[32,40,128]{2,1,0:T(8,128)(2,1)}), bf16[32,40,128]{2,1,0:T(8,128)(2,1)S(1)}, u32[]{:S(2)}, u32[]{:S(2)}) %all-to-all-start.1) | async-done | bytes 327712 | tf_op jit(solution)/shard_map/all_to_all | solution.py:520
  62.8 7.3 %shard_map.98 = (bf16[128,2048]{1,0:T(8,128)(2,1)}, bf16[128,2048]{1,0:T(8,128)(2,1)}, f32[32,4096]{1,0:T(8,128)}) custom-call(f32[1,32]{1,0:T(1,128)} %rate_hbm.5, bf16[32,40,128]{2,1,0:T(8,128)(2,1)S(1)} %all-to-all-done.1.code_ref, bf16[256,2048]{1,0:T(8,128)(2,1)S(1)} %get-tuple-element.29.e_ref, bf16[256,2048]{1,0:T(8,128)(2,1)S(1)} %get-tuple-element.32.wt_ref, ...), custom_call_target="tpu_custom_call" | custom-call | flops 1342177280 | bytes 8716416 | tf_op jit(solution)/shard_map/pallas_call | solution.py:445
Async XLA Ops:
  0.6 7.4 %collective-permute-start = (bf16[1,128,2048]{2,1,0:T(8,128)(2,1)}, bf16[1,128,2048]{2,1,0:T(8,128)(2,1)S(1)}, u32[]{:S(2)}, u32[]{:S(2)}) collective-permute-start(bf16[1,128,2048]{2,1,0:T(8,128)(2,1)} %param.9), channel_id=1, source_target_pairs={{32,0},{64,32},{96,64},{128,96},{160,128},{192,160},{224,192},{0,2... | collective-permute-start | bytes 1572872 | tf_op jit(solution)/shard_map/ppermute | solution.py:487
  8.0 1.5 %copy-start = (bf16[1,128,2048]{2,1,0:T(8,128)(2,1)}, bf16[1,128,2048]{2,1,0:T(8,128)(2,1)S(1)}, u32[]{:S(2)}) copy-start(bf16[1,128,2048]{2,1,0:T(8,128)(2,1)S(1)} %collective-permute-done) | copy-start | bytes 1572868
  9.6 31.2 %all-to-all-start = ((bf16[32,72,128]{2,1,0:T(8,128)(2,1)}), bf16[32,72,128]{2,1,0:T(8,128)(2,1)S(1)}, u32[]{:S(2)}, u32[]{:S(2)}) async-start(bf16[32,72,128]{2,1,0:T(8,128)(2,1)} %shard_map.94), calls=%async_computation | async-start | bytes 1179648 | tf_op jit(solution)/shard_map/all_to_all | solution.py:500
  43.7 19.1 %all-to-all-start.1 = ((bf16[32,40,128]{2,1,0:T(8,128)(2,1)}), bf16[32,40,128]{2,1,0:T(8,128)(2,1)S(1)}, u32[]{:S(2)}, u32[]{:S(2)}) async-start(bf16[32,40,128]{2,1,0:T(8,128)(2,1)} %shard_map.96), calls=%async_computation.1 | async-start | bytes 655360 | tf_op jit(solution)/shard_map/all_to_all | solution.py:520

commit v5 on v4

--- a/solution.py
+++ b/solution.py
@@ -134,6 +134,11 @@
     if ship is not None:
         for i in range(CHUNKS):
             ship[1](i)
+
+
+def part_copy(source, target, sems, i):
+    size = source.shape[0] // CHUNKS
+    return pltpu.make_async_copy(source.at[pl.ds(i * size, size)], target.at[pl.ds(i * size, size)], sems.at[i])
 
 
 def map_kernel(rate_hbm, q_hbm, k_hbm, acode_ref, ascale_ref, mt_ref, rate_ref, rate_sem, q_ref, k_ref, in_sems):
@@ -177,7 +182,7 @@
     run(work, features // QUAD, fetch, None, pltpu.make_async_copy(rate_hbm, rate_ref, rate_sem))
 
 
-def pack_kernel(mt_ref, dz_ref, acode_ref, ascale_ref, out_ref):
+def pack_kernel(mt_ref, dz_ref, acode_ref, ascale_ref, out_hbm, out_ref, sems):
     masks = head_masks()
     left = lax.broadcasted_iota(jnp.int32, (DH, 128), 1) < DH
     left8 = left[:8]
@@ -198,11 +203,16 @@
             out_ref[head + 1, 0:DH, :] = jnp.where(left, pltpu.roll(a_code[:, cut], DH, 1), code[:, cut]).astype(BF16)
             out_ref[head + 1, DH : DH + 8, :] = jnp.where(left8, pltpu.roll(a_scale[:, cut], DH, 1), scale[:, cut]).astype(BF16)
 
-    for index in range(dz_ref.shape[1] // QUAD):
+    each = dz_ref.shape[1] // QUAD // CHUNKS
+    for index in range(each * CHUNKS):
         work(index, slice(index * QUAD, (index + 1) * QUAD))
-
-
-def relay_kernel(in_ref, out_ref, map_ref, left_ref, group):
+        if index % each == each - 1:
+            part_copy(out_ref, out_hbm, sems, index // each).start()
+    for i in range(CHUNKS):
+        part_copy(out_ref, out_hbm, sems, i).wait()
+
+
+def relay_kernel(in_ref, out_hbm, out_ref, map_ref, left_ref, sems, group):
     shards = in_ref.shape[0]
     row = lax.broadcasted_iota(jnp.int32, (DH, 128), 0)
     lane = lax.broadcasted_iota(jnp.int32, (DH, 128), 1)
@@ -281,6 +291,11 @@
             out_ref[j, half : half + 8, :] = jnp.where(left[:8], scale, other).astype(BF16)
             out_ref[j + 1, 0:half, :] = jnp.where(low, turned[:half], code[half:]).astype(BF16)
             out_ref[j + 1, half : half + 8, :] = jnp.where(left[:8], other, scale).astype(BF16)
+        size = shards // CHUNKS
+        if (g + 1) * group % size == 0:
+            part_copy(out_ref, out_hbm, sems, ((g + 1) * group - 1) // size).start()
+    for i in range(CHUNKS):
+        part_copy(out_ref, out_hbm, sems, i).wait()
 
 
 def trail_kernel(rate_hbm, *refs):
@@ -494,8 +509,14 @@
         rate + buffers([q, k]) + [semaphores(2)],
         MAP_LIMIT,
     )
+    sent, back = jax.ShapeDtypeStruct((heads, DH + 8, 128), BF16), jax.ShapeDtypeStruct((shards, DH // 2 + 8, 128), BF16)
     (packed,) = call(
-        pack_kernel, inside([mt, dz, acode, ascale]), inside([jax.ShapeDtypeStruct((heads, DH + 8, 128), BF16)]), 2 * unit, (), 24
+        pack_kernel,
+        inside([mt, dz, acode, ascale]),
+        outside([sent]),
+        2 * unit,
+        buffers([sent]) + [pltpu.SemaphoreType.DMA((CHUNKS,))],
+        24,
     )
     arrived = lax.all_to_all(packed, "seq", 0, 0, tiled=True)
     rate_later, _ = lax.optimization_barrier((inner_rate, packed))
@@ -512,9 +533,9 @@
     (ends,) = call(
         partial(relay_kernel, group=4),
         inside([arrived]),
-        inside([jax.ShapeDtypeStruct((shards, DH // 2 + 8, 128), BF16)]),
+        outside([back]),
         unit,
-        [pltpu.VMEM((shards, DH, 128), F32), pltpu.VMEM((shards, DH, 256), BF16)],
+        buffers([back]) + [pltpu.VMEM((shards, DH, 128), F32), pltpu.VMEM((shards, DH, 256), BF16), pltpu.SemaphoreType.DMA((CHUNKS,))],
         24,
     )
     returned = lax.all_to_all(ends, "seq", 0, 0, tiled=True)

time: 70.5 us -> 70.4 us (level)
  no operation moved by 1% of the time
where the time goes in v5:
time: 70.4 us; the launch traced here: 70 us
  Pallas kernels  38 us (54%)
  starting transfers between devices  16.5 us (23%)
  waiting for transfers between devices  14.8 us (21%)
  between operations  0.72 us (1%)
    pallas_call x6, Pallas kernels, call(): pl.pallas_call(kernel, out_shape=tuple((shape if memory is pltpu.VMEM els...  38 us
    all_to_all x1, starting transfers between devices, per_device(): arrived = lax.all_to_all(packed, 'seq', 0, 0, tiled=True)  11.2 us
    all_to_all x1, waiting for transfers between devices, per_device(): arrived = lax.all_to_all(packed, 'seq', 0, 0, tiled=True)  8.05 us
    all_to_all x1, waiting for transfers between devices, per_device(): returned = lax.all_to_all(ends, 'seq', 0, 0, tiled=True)  6.75 us
    all_to_all x1, starting transfers between devices, per_device(): returned = lax.all_to_all(ends, 'seq', 0, 0, tiled=True)  5.24 us
  transfers between devices with their start and end apart: 3, of which 2 were waited for; matrix products, arithmetic and copies ran while one was open for 0% of the time, Pallas kernels for 38%

profile of v5, /device:TPU:40, one launch (start us, length us, event | category | flops | bytes accessed | tf_op | source)
XLA Modules:
  0.0 70.0 jit_solution(8699837121182490905)
XLA Ops:
  0.6 0.0 collective-permute-start
  0.7 7.3 %shard_map.93 = (bf16[64,2048]{1,0:T(8,128)(2,1)S(1)}, f32[8,2048]{1,0:T(8,128)S(1)}, bf16[256,2048]{1,0:T(8,128)(2,1)S(1)}) custom-call(f32[1,32]{1,0:T(1,128)} %rate_hbm.5, bf16[128,2048]{1,0:T(8,128)(2,1)} %bitcast.18, bf16[128,2048]{1,0:T(8,128)(2,1)} %bitcast.12), custom_call_target="tpu_custom_call" | custom-call | flops 1073741824 | bytes 2424960 | tf_op jit(solution)/shard_map/pallas_call | solution.py:460
  8.0 0.0 collective-permute-done
  8.0 0.0 copy-start
  8.0 1.4 %shard_map.94 = bf16[32,72,128]{2,1,0:T(8,128)(2,1)} custom-call(bf16[256,2048]{1,0:T(8,128)(2,1)S(1)} %get-tuple-element.22.mt_ref, bf16[128,2048]{1,0:T(8,128)(2,1)S(1)} %bitcast.9, bf16[64,2048]{1,0:T(8,128)(2,1)S(1)} %get-tuple-element.23.acode_ref, f32[8,2048]{1,0:T(8,128)S(1)} %get-tuple-element.24.ascale_ref), custom_call_target="tpu_custom_call" | custom-call | flops 268435456 | bytes 2490368 | tf_op jit(solution)/shard_map/pallas_call | solution.py:460
  9.4 0.0 copy-done
  9.4 11.2 %all-to-all-start = ((bf16[32,72,128]{2,1,0:T(8,128)(2,1)}), bf16[32,72,128]{2,1,0:T(8,128)(2,1)S(1)}, u32[]{:S(2)}, u32[]{:S(2)}) async-start(bf16[32,72,128]{2,1,0:T(8,128)(2,1)} %shard_map.94), calls=%async_computation | async-start | bytes 1179648 | tf_op jit(solution)/shard_map/all_to_all | solution.py:521
  20.7 12.0 %shard_map.95 = (bf16[256,2048]{1,0:T(8,128)(2,1)S(1)}, bf16[1024,512]{1,0:T(8,128)(2,1)}, bf16[1024,512]{1,0:T(8,128)(2,1)}, f32[512,512]{1,0:T(8,128)}, f32[512,512]{1,0:T(8,128)}) custom-call(f32[1,32]{1,0:T(1,128)} %rate_hbm.5, bf16[128,2048]{1,0:T(8,128)(2,1)} %bitcast.19, bf16[128,2048]{1,0:T(8,128)(2,1)} %bitcast.13, bf16[128,2048]{1,0:T(8,128)(2,1)} %bitcast.16, ...), custom_call_target="tpu_custom_call" | custom-call | flops 1342177280 | bytes 7864448 | tf_op jit(solution)/shard_map/pallas_call | solution.py:460
  32.6 8.1 %all-to-all-done.in_ref = bf16[32,72,128]{2,1,0:T(8,128)(2,1)S(1)} async-done(((bf16[32,72,128]{2,1,0:T(8,128)(2,1)}), bf16[32,72,128]{2,1,0:T(8,128)(2,1)S(1)}, u32[]{:S(2)}, u32[]{:S(2)}) %all-to-all-start) | async-done | bytes 589856 | tf_op jit(solution)/shard_map/all_to_all | solution.py:521
  40.7 2.9 %shard_map.96 = bf16[32,40,128]{2,1,0:T(8,128)(2,1)} custom-call(bf16[32,72,128]{2,1,0:T(8,128)(2,1)S(1)} %all-to-all-done.in_ref), custom_call_target="tpu_custom_call" | custom-call | flops 134217728 | bytes 917504 | tf_op jit(solution)/shard_map/pallas_call | solution.py:460
  43.6 5.2 %all-to-all-start.1 = ((bf16[32,40,128]{2,1,0:T(8,128)(2,1)}), bf16[32,40,128]{2,1,0:T(8,128)(2,1)S(1)}, u32[]{:S(2)}, u32[]{:S(2)}) async-start(bf16[32,40,128]{2,1,0:T(8,128)(2,1)} %shard_map.96), calls=%async_computation.1 | async-start | bytes 655360 | tf_op jit(solution)/shard_map/all_to_all | solution.py:541
  48.8 7.1 %shard_map.97 = (bf16[128,2048]{1,0:T(8,128)(2,1)}, f32[512,512]{1,0:T(8,128)}, bf16[256,2048]{1,0:T(8,128)(2,1)S(1)}) custom-call(f32[1,32]{1,0:T(1,128)} %rate_hbm.5, bf16[256,2048]{1,0:T(8,128)(2,1)S(1)} %get-tuple-element.29.e_ref, bf16[128,2048]{1,0:T(8,128)(2,1)} %bitcast.20, bf16[128,2048]{1,0:T(8,128)(2,1)} %bitcast.14, bf16[128,2048]{1,0:T(8,128)(2,1)} %bitcast.11, ...), custom_call_target="tpu_custom_call" | custom-call | flops 1342177280 | bytes 6291584 | tf_op jit(solution)/shard_map/pallas_call | solution.py:460
  56.0 6.8 %all-to-all-done.1.code_ref = bf16[32,40,128]{2,1,0:T(8,128)(2,1)S(1)} async-done(((bf16[32,40,128]{2,1,0:T(8,128)(2,1)}), bf16[32,40,128]{2,1,0:T(8,128)(2,1)S(1)}, u32[]{:S(2)}, u32[]{:S(2)}) %all-to-all-start.1) | async-done | bytes 327712 | tf_op jit(solution)/shard_map/all_to_all | solution.py:541
  62.7 7.3 %shard_map.98 = (bf16[128,2048]{1,0:T(8,128)(2,1)}, bf16[128,2048]{1,0:T(8,128)(2,1)}, f32[32,4096]{1,0:T(8,128)}) custom-call(f32[1,32]{1,0:T(1,128)} %rate_hbm.5, bf16[32,40,128]{2,1,0:T(8,128)(2,1)S(1)} %all-to-all-done.1.code_ref, bf16[256,2048]{1,0:T(8,128)(2,1)S(1)} %get-tuple-element.29.e_ref, bf16[256,2048]{1,0:T(8,128)(2,1)S(1)} %get-tuple-element.32.wt_ref, ...), custom_call_target="tpu_custom_call" | custom-call | flops 1342177280 | bytes 8716416 | tf_op jit(solution)/shard_map/pallas_call | solution.py:460
Async XLA Ops:
  0.6 7.4 %collective-permute-start = (bf16[1,128,2048]{2,1,0:T(8,128)(2,1)}, bf16[1,128,2048]{2,1,0:T(8,128)(2,1)S(1)}, u32[]{:S(2)}, u32[]{:S(2)}) collective-permute-start(bf16[1,128,2048]{2,1,0:T(8,128)(2,1)} %param.9), channel_id=1, source_target_pairs={{32,0},{64,32},{96,64},{128,96},{160,128},{192,160},{224,192},{0,2... | collective-permute-start | bytes 1572872 | tf_op jit(solution)/shard_map/ppermute | solution.py:502
  8.0 1.4 %copy-start = (bf16[1,128,2048]{2,1,0:T(8,128)(2,1)}, bf16[1,128,2048]{2,1,0:T(8,128)(2,1)S(1)}, u32[]{:S(2)}) copy-start(bf16[1,128,2048]{2,1,0:T(8,128)(2,1)S(1)} %collective-permute-done) | copy-start | bytes 1572868
  9.4 31.2 %all-to-all-start = ((bf16[32,72,128]{2,1,0:T(8,128)(2,1)}), bf16[32,72,128]{2,1,0:T(8,128)(2,1)S(1)}, u32[]{:S(2)}, u32[]{:S(2)}) async-start(bf16[32,72,128]{2,1,0:T(8,128)(2,1)} %shard_map.94), calls=%async_computation | async-start | bytes 1179648 | tf_op jit(solution)/shard_map/all_to_all | solution.py:521
  43.6 19.1 %all-to-all-start.1 = ((bf16[32,40,128]{2,1,0:T(8,128)(2,1)}), bf16[32,40,128]{2,1,0:T(8,128)(2,1)S(1)}, u32[]{:S(2)}, u32[]{:S(2)}) async-start(bf16[32,40,128]{2,1,0:T(8,128)(2,1)} %shard_map.96), calls=%async_computation.1 | async-start | bytes 655360 | tf_op jit(solution)/shard_map/all_to_all | solution.py:541
